TPU v7x, 128 devices: a whole 4x4x4 slice. The times are simulated.
128 devices in a mesh: shard: 4 (over y_lo, core), replica: 32 (over z, x, y_hi).
Axes of the slice: x: 4, y: 4 (y_hi: 2, y_lo: 2; y = y_hi * 2 + y_lo), z: 4, core: 2. Of those that a mesh axis runs over, the one named last changes fastest.
Arguments:
- tokens: bfloat16 [128, 384, 960], P(('shard', 'replica')), may hold values from -6 to 6
- lengths: int32 [128, 4], P(('shard', 'replica')), may hold values from 0 to 384, as said below
- norm_attn: bfloat16 [960], P('shard'), may hold values from 0.5 to 1.5
- w_query: bfloat16 [960, 960], P('shard'), may hold values from -0.1875 to 0.1875
- w_key: bfloat16 [960, 320], P('shard'), may hold values from -0.1875 to 0.1875
- w_value: bfloat16 [960, 320], P('shard'), may hold values from -0.1875 to 0.1875
- w_out: bfloat16 [960, 960], P('shard'), may hold values from -2 to 2
- norm_mlp: bfloat16 [960], P('shard'), may hold values from 0.5 to 1.5
- w_gate: bfloat16 [960, 2560], P('shard'), may hold values from -0.1875 to 0.1875
- w_up: bfloat16 [960, 2560], P('shard'), may hold values from -0.1875 to 0.1875
- w_down: bfloat16 [2560, 960], P('shard'), may hold values from -0.125 to 0.125
- cotangent: bfloat16 [128, 384, 960], P(('shard', 'replica')), may hold values from -6 to 6
Outputs:
- out: bfloat16 [128, 384, 960], P(('shard', 'replica'))
- grad_in: float32 [128, 384, 960], P(('shard', 'replica'))
- grad_norm_attn: float32 [960], P('shard')
- grad_query: float32 [960, 960], P('shard')
- grad_key: float32 [960, 320], P('shard')
- grad_value: float32 [960, 320], P('shard')
- grad_out_proj: float32 [960, 960], P('shard')
- grad_norm_mlp: float32 [960], P('shard')
- grad_gate: float32 [960, 2560], P('shard')
- grad_up: float32 [960, 2560], P('shard')
- grad_down: float32 [2560, 960], P('shard')
Inputs may be any that keep to these rules, and one draw needn't show every extreme that they name: Row g lists the lengths of the sequences packed in order into pack g's 384 slots, zeros for unused entries; each row sums to 384.
All inputs are finite; a program needn't handle non-finite values.
Results may differ from a plain program's by a relative error of at most 0.028.
Values may be sent and summed in bfloat16 or wider, within the bound.
No kernel may reach another device: no remote copies, remote signals or barrier semaphores. Data moves between devices by JAX's collectives and lax.ppermute only.
A program may use at most 256 MiB of HBM per device.

v0:
```python
import jax
import jax.numpy as jnp
from jax import lax
from jax.sharding import Mesh
from jax.sharding import PartitionSpec as P

HEADS = 15
KV_HEADS = 5
HEAD_DIM = 64
SHARD_REPLICA = ("shard", "replica_0", "replica_1", "replica_2")
REPLICA = ("replica_0", "replica_1", "replica_2")


EPS = 1e-05
BASE = 100000.0
MASKED = -1e30


def sent_together(arrays, axis, dim, along):
    columns = [a.reshape(*a.shape[:along], -1) for a in arrays]
    both = jnp.concatenate(columns, axis=along)
    out, at, outs = (lax.all_gather(both, axis, axis=dim, tiled=True), 0, [])
    for a, column in zip(arrays, columns):
        section = out[..., at : at + column.shape[along]]
        outs.append(section.reshape(*section.shape[:along], *a.shape[along:]))
        at += column.shape[along]
    return tuple(outs)


def gathered_total(shard, axis):
    return lax.all_gather(shard, axis).sum(0)


def for_sending(shard):
    return jax.tree.map(lambda a: a.astype(jnp.bfloat16) if a.dtype == jnp.float32 else a, shard)


def joined_along(parts, dim):
    lengths = list(parts.shape[1:])
    lengths[dim] *= parts.shape[0]
    return jnp.moveaxis(parts, 0, dim).reshape(lengths)


def stacked_from(shard, axes, turns):
    parts = shard
    for k in turns:
        parts = lax.all_gather(parts, axes[k])
    done = turns[::-1]
    back = [done.index(k) for k in range(len(axes))]
    parts = parts.transpose(*back, *range(len(axes), parts.ndim))
    return parts.reshape(-1, *shard.shape)


def gather_axes(shard, axes, turns, dim):
    return joined_along(stacked_from(shard, axes, turns), dim)


def slots_of(lengths_row, total):
    slots = jnp.arange(total, dtype=jnp.int32)
    ends = jnp.cumsum(lengths_row)
    reached = slots[:, None] >= ends[None, :]
    segment = jnp.sum(reached.astype(jnp.int32), axis=1)
    start = jnp.max(jnp.where(reached, ends[None, :], 0), axis=1)
    return (segment, slots - start, slots)


def rotate(values, position, sign):
    half = values.shape[-1] // 2
    freq = BASE ** (-jnp.arange(half, dtype=jnp.float32) * 2.0 / values.shape[-1])
    angle = position.astype(jnp.float32)[:, None] * freq[None, :]
    cosine = jnp.cos(angle)[:, None, :]
    sine = sign * jnp.sin(angle)[:, None, :]
    first = values[..., :half]
    second = values[..., half:]
    return jnp.concatenate(
        [first * cosine - second * sine, second * cosine + first * sine], axis=-1
    )


def normed(values, gain):
    scale = lax.rsqrt(jnp.mean(values * values, axis=-1, keepdims=True) + EPS)
    return (values * scale * gain, scale)


def norm_back(values, scale, gain, grad):
    inner = grad * gain
    cubed = scale * scale * scale
    d_values = scale * inner - values * cubed * jnp.mean(values * inner, axis=-1, keepdims=True)
    d_gain = jnp.sum(grad * values * scale, axis=0)
    return (d_values, d_gain)


def mult(left, right):
    return jnp.dot(left, right, preferred_element_type=jnp.float32)


def mult_tn(left, right):
    return lax.dot_general(
        left, right, (((0,), (0,)), ((), ())), preferred_element_type=jnp.float32
    )


def mult_nt(left, right):
    return lax.dot_general(
        left, right, (((1,), (1,)), ((), ())), preferred_element_type=jnp.float32
    )


def body(
    tokens,
    lengths,
    norm_attn,
    w_query,
    w_key,
    w_value,
    w_out,
    norm_mlp,
    w_gate,
    w_up,
    w_down,
    cotangent,
):
    shards = lax.axis_size("shard")
    me = lax.axis_index("shard")
    local = tokens.shape[1]
    width = tokens.shape[2]
    group_size = HEADS // KV_HEADS
    pieces = (norm_attn, w_query, w_key, w_value, w_out, norm_mlp, w_gate, w_up, w_down)
    full = (
        *sent_together(
            (
                pieces[0],
                pieces[1],
                pieces[2],
                pieces[3],
                pieces[4],
                pieces[5],
                pieces[6],
                pieces[7],
            ),
            "shard",
            0,
            1,
        ),
        lax.all_gather(pieces[8], "shard", axis=0, tiled=True),
    )
    gain_attn, wq, wk, wv, wo, gain_mlp, wg, wu, wd = full
    gain_attn = gain_attn.astype(jnp.float32)
    gain_mlp = gain_mlp.astype(jnp.float32)
    segment, position, slots = slots_of(lengths[0], local)
    allowed = (segment[:, None] == segment[None, :]) & (slots[None, :] <= slots[:, None])
    x = tokens[0].astype(jnp.float32)
    a_full, scale_a = normed(x, gain_attn)
    a_low = a_full.astype(jnp.bfloat16)
    query = rotate(mult(a_low, wq).reshape(local, HEADS, HEAD_DIM), position, 1.0).astype(
        jnp.bfloat16
    )
    keys = rotate(mult(a_low, wk).reshape(local, KV_HEADS, HEAD_DIM), position, 1.0).astype(
        jnp.bfloat16
    )
    values = mult(a_low, wv).astype(jnp.bfloat16)
    query_heads = query.reshape(local, KV_HEADS, group_size, HEAD_DIM).transpose(1, 0, 2, 3)
    key_heads = keys.transpose(1, 0, 2)
    value_heads = values.reshape(local, KV_HEADS, HEAD_DIM).transpose(1, 0, 2)

    def head_scores(query_one, key_one):
        scores = (
            jnp.einsum("tgd,sd->gts", query_one, key_one, preferred_element_type=jnp.float32)
            * 0.125
        )
        return jnp.where(allowed[None], scores, MASKED)

    def head_forward(item):
        query_one, key_one, value_one = item
        scores = head_scores(query_one, key_one)
        top = jnp.max(scores, axis=-1, keepdims=True)
        expo = jnp.exp(scores - top)
        total_weight = jnp.sum(expo, axis=-1, keepdims=True)
        prob_low = (expo / total_weight).astype(jnp.bfloat16)
        result = jnp.einsum("gts,sd->tgd", prob_low, value_one, preferred_element_type=jnp.float32)
        return (result, top + jnp.log(total_weight))

    attended, log_total = lax.map(head_forward, (query_heads, key_heads, value_heads))
    att_low = attended.transpose(1, 0, 2, 3).reshape(local, HEADS * HEAD_DIM).astype(jnp.bfloat16)
    hidden = x + mult(att_low, wo)
    b_full, scale_b = normed(hidden, gain_mlp)
    b_low = b_full.astype(jnp.bfloat16)
    gate = mult(b_low, wg)
    upper = mult(b_low, wu)
    sigma = jax.nn.sigmoid(gate)
    silu_gate = gate * sigma
    act_low = (silu_gate * upper).astype(jnp.bfloat16)
    result = (hidden + mult(act_low, wd)).astype(jnp.bfloat16)[None]
    _, wq, wk, wv, wo, _, wg, wu, wd = full
    dy_low = cotangent[0]
    dy = dy_low.astype(jnp.float32)
    grad_down = mult_tn(act_low, dy_low)
    d_act = mult_nt(dy_low, wd)
    d_gate = (d_act * upper * sigma * (1.0 + gate * (1.0 - sigma))).astype(jnp.bfloat16)
    d_up = (d_act * silu_gate).astype(jnp.bfloat16)
    grad_gate = mult_tn(b_low, d_gate)
    grad_up = mult_tn(b_low, d_up)
    d_b = mult_nt(d_gate, wg) + mult_nt(d_up, wu)
    d_hidden_norm, grad_gain_mlp = norm_back(hidden, scale_b, gain_mlp, d_b)
    d_hidden = dy + d_hidden_norm
    d_hidden_low = d_hidden.astype(jnp.bfloat16)
    grad_out_proj = mult_tn(att_low, d_hidden_low)
    d_att = mult_nt(d_hidden_low, wo).astype(jnp.bfloat16)
    d_att_heads = d_att.reshape(local, KV_HEADS, group_size, HEAD_DIM).transpose(1, 0, 2, 3)

    def head_backward(item):
        query_one, key_one, value_one, d_one, log_one = item
        prob = jnp.exp(head_scores(query_one, key_one) - log_one)
        prob_low = prob.astype(jnp.bfloat16)
        d_prob = jnp.einsum("tgd,sd->gts", d_one, value_one, preferred_element_type=jnp.float32)
        inner = jnp.sum(prob * d_prob, axis=-1, keepdims=True)
        d_scores = (prob * (d_prob - inner)).astype(jnp.bfloat16)
        d_query = (
            jnp.einsum("gts,sd->tgd", d_scores, key_one, preferred_element_type=jnp.float32) * 0.125
        )
        d_key = (
            jnp.einsum("gts,tgd->sd", d_scores, query_one, preferred_element_type=jnp.float32)
            * 0.125
        )
        d_value = jnp.einsum("gts,tgd->sd", prob_low, d_one, preferred_element_type=jnp.float32)
        return (d_query, d_key, d_value)

    d_query, d_keys, d_values = lax.map(
        head_backward, (query_heads, key_heads, value_heads, d_att_heads, log_total)
    )
    dq_low = rotate(d_query.transpose(1, 0, 2, 3).reshape(local, HEADS, HEAD_DIM), position, -1.0)
    dq_low = dq_low.reshape(local, HEADS * HEAD_DIM).astype(jnp.bfloat16)
    dk_low = rotate(d_keys.transpose(1, 0, 2), position, -1.0)
    dk_low = dk_low.reshape(local, KV_HEADS * HEAD_DIM).astype(jnp.bfloat16)
    dv_low = d_values.transpose(1, 0, 2).reshape(local, KV_HEADS * HEAD_DIM).astype(jnp.bfloat16)
    grad_query = mult_tn(a_low, dq_low)
    grad_key = mult_tn(a_low, dk_low)
    grad_value = mult_tn(a_low, dv_low)
    d_a = mult_nt(dq_low, wq) + mult_nt(dk_low, wk) + mult_nt(dv_low, wv)
    d_x_norm, grad_gain_attn = norm_back(x, scale_a, gain_attn, d_a)
    grad_input = (d_hidden + d_x_norm)[None]
    gains = (
        gathered_total(grad_gain_attn, SHARD_REPLICA),
        gathered_total(grad_gain_mlp, SHARD_REPLICA),
    )
    gain_rows = width // shards
    owned_attn = lax.dynamic_slice_in_dim(gains[0], me * gain_rows, gain_rows)
    owned_mlp = lax.dynamic_slice_in_dim(gains[1], me * gain_rows, gain_rows)
    count = shards * lax.axis_size(REPLICA)
    matrices = (grad_query, grad_key, grad_value, grad_out_proj, grad_gate, grad_up, grad_down)
    summed = lax.psum_scatter(
        tuple((m.reshape(count, -1) for m in matrices)),
        SHARD_REPLICA,
        scatter_dimension=0,
        tiled=True,
    )
    owned = jax.tree.map(
        lambda part, own: part.astype(own.dtype),
        jax.tree.map(lambda part: gather_axes(part, REPLICA, (2, 0, 1), 0), for_sending(summed)),
        summed,
    )
    shaped = [o.reshape(m.shape[0] // shards, m.shape[1]) for o, m in zip(owned, matrices)]
    result_grads = (
        owned_attn,
        shaped[0],
        shaped[1],
        shaped[2],
        shaped[3],
        owned_mlp,
        shaped[4],
        shaped[5],
        shaped[6],
    )
    return (
        result,
        grad_input,
        result_grads[0],
        result_grads[1],
        result_grads[2],
        result_grads[3],
        result_grads[4],
        result_grads[5],
        result_grads[6],
        result_grads[7],
        result_grads[8],
    )


def solution(mesh):
    torus = Mesh(
        mesh.devices.reshape(mesh.shape["shard"], 4, 4, 2),
        ("shard", "replica_0", "replica_1", "replica_2"),
    )
    return jax.shard_map(
        body,
        mesh=torus,
        in_specs=(
            P(SHARD_REPLICA, None, None),
            P(SHARD_REPLICA, None),
            P("shard"),
            P("shard", None),
            P("shard", None),
            P("shard", None),
            P("shard", None),
            P("shard"),
            P("shard", None),
            P("shard", None),
            P("shard", None),
            P(SHARD_REPLICA, None, None),
        ),
        out_specs=(
            P(SHARD_REPLICA, None, None),
            P(SHARD_REPLICA, None, None),
            P("shard"),
            P("shard", None),
            P("shard", None),
            P("shard", None),
            P("shard", None),
            P("shard"),
            P("shard", None),
            P("shard", None),
            P("shard", None),
        ),
        check_vma=False,
    )
```

profile of v0, /device:TPU:0, one launch (start us, length us, event | category | flops | bytes accessed | tf_op | source)
XLA Modules:
  0.0 917.0 jit_solution(1700943435393089581)
XLA Ops:
  10.8 7.4 concatenate.22
  21.1 43.0 %all-gather.45.cloned.1.call-done = bf16[2560,960]{0,1:T(8,128)(2,1)} async-done(((bf16[640,960]{0,1:T(8,128)(2,1)}), bf16[2560,960]{0,1:T(8,128)(2,1)}) %all-gather.45.cloned.1.call-update) | async-done | bytes 4915216 | tf_op jit(solution)/shard_map/all_gather | solution.py:145
  64.1 6.5 fusion.93
  70.6 131.0 %all-gather.43.cloned.1.call-done = bf16[960,7682]{1,0:T(8,128)(2,1)} async-done(((bf16[240,7682]{1,0:T(8,128)(2,1)}), bf16[960,7682]{1,0:T(8,128)(2,1)}) %all-gather.43.cloned.1.call-update) | async-done | bytes 14749456 | tf_op jit(solution)/shard_map/all_gather | solution.py:22
  216.5 10.0 %while.30 = (s32[]{:T(128)}, bf16[5,384,3,64]{1,3,2,0:T(8,128)(2,1)S(1)}, f32[5,3,384,1]{2,1,3,0:T(4,128)}, bf16[5,384,64]{1,2,0:T(8,128)(2,1)S(1)}, bf16[5,384,...) while((s32[]{:T(128)}, ...), condition=%wide.region_7.8_spmd.clone.clone, body=%wide.region_4.7_spmd.clone.sunk.clone | while | flops 117226368 | bytes 6189145 | solution.py:183
  226.6 4.1 multiply_reduce_fusion.2
  231.0 5.3 fusion.50
  236.3 8.0 multiply_convert_fusion.1
  244.4 5.1 fusion.127
  249.5 5.1 fusion.128
  254.7 5.1 fusion.48
  259.8 6.1 multiply_reduce_fusion
  270.2 3.7 fusion.86
  273.9 32.9 %while.31 = (s32[]{:T(128)}, f32[5,384,3,64]{1,3,2,0:T(8,128)}, f32[5,384,64]{1,2,0:T(8,128)}, bf16[5,384,64]{1,2,0:T(8,128)(2,1)S(1)}, bf16[5,384,64]{1,2,0:T(8...) while((s32[]{:T(128)}, f32[5,384,3,64]{1,3,2,0:T(8,128)}, ...), condition=%wide.region_12.13_spmd.clone.clone, body=%wide.region_10.12_spmd.clone.sunk.clone | while | flops 287636352 | bytes 14826097 | solution.py:228
  319.3 5.8 reshape.388
  329.3 5.8 reshape.385
  335.1 11.7 %reshape.389 = f32[128,19200]{1,0:T(8,128)} reshape(f32[960,2560]{1,0:T(8,128)} %fusion.127) | data formatting | bytes 19660800 | tf_op jit(solution)/shard_map/reshape | solution.py:252
  346.8 11.7 %reshape.390 = f32[128,19200]{1,0:T(8,128)} reshape(f32[960,2560]{1,0:T(8,128)} %fusion.128) | data formatting | bytes 19660800 | tf_op jit(solution)/shard_map/reshape | solution.py:252
  358.5 7.1 fusion.91
  365.6 12.2 %reshape.391 = f32[128,19200]{1,0:T(8,128)} reshape(f32[2560,960]{1,0:T(8,128)} %fusion.91) | data formatting | bytes 19660800 | tf_op jit(solution)/shard_map/reshape | solution.py:252
  377.8 222.8 %all-reduce.15 = (bf16[128,7200]{1,0:T(8,128)(2,1)}, bf16[128,2400]{1,0:T(8,128)(2,1)}, bf16[128,2400]{1,0:T(8,128)(2,1)}, bf16[128,7200]{1,0:T(8,128)(2,1)}, bf...) all-reduce(f32[128,7200]{1,0:T(8,128)} %reshape.385, ...), channel_id=25, replica_groups=mesh['shard'=4,'replica_0'=4,'replica_1'=4,'replica_2'=2] {'shard','repl..., use_global_device_ids=true, to_apply=%region_16.17.clone | all-reduce | flops 9830400 | bytes 58982400
  602.4 5.9 all-gather.25
  609.1 5.9 all-gather.27
  615.0 11.9 %all-gather.28 = bf16[4,2,2400]{2,1,0:T(2,128)(2,1)S(1)} all-gather(bf16[1,2,2400]{2,1,0:T(2,128)(2,1)S(1)} %bitcast.399), channel_id=10, replica_groups=mesh['shard'=4,'replica_0'=4,'replica_1'=4,'replica_2'=2] {'replica_0'}, dimensions={0}, use_global_device_ids=true | all-gather | bytes 48000 | tf_op jit(solution)/shard_map/all_gather | solution.py:47
  626.9 11.9 %all-gather.26 = bf16[4,2,2400]{2,1,0:T(2,128)(2,1)S(1)} all-gather(bf16[1,2,2400]{2,1,0:T(2,128)(2,1)S(1)} %bitcast.398), channel_id=7, replica_groups=mesh['shard'=4,'replica_0'=4,'replica_1'=4,'replica_2'=2] {'replica_0'}, dimensions={0}, use_global_device_ids=true | all-gather | bytes 48000 | tf_op jit(solution)/shard_map/all_gather | solution.py:47
  645.4 12.8 %all-gather.6 = bf16[16,2,1,2400]{3,1,2,0:T(2,128)(2,1)} all-gather(bf16[4,2,1,2400]{3,1,2,0:T(2,128)(2,1)S(1)} %bitcast.395), channel_id=8, replica_groups=mesh['shard'=4,'replica_0'=4,'replica_1'=4,'replica_2'=2] {'replica_1'}, dimensions={0}, use_global_device_ids=true | all-gather | bytes 192000 | tf_op jit(solution)/shard_map/all_gather | solution.py:47
  658.2 12.0 %all-gather.9 = bf16[16,2,1,2400]{3,1,2,0:T(2,128)(2,1)S(1)} all-gather(bf16[4,2,1,2400]{3,1,2,0:T(2,128)(2,1)S(1)} %bitcast.394), channel_id=11, replica_groups=mesh['shard'=4,'replica_0'=4,'replica_1'=4,'replica_2'=2] {'replica_1'}, dimensions={0}, use_global_device_ids=true | all-gather | bytes 192000 | tf_op jit(solution)/shard_map/all_gather | solution.py:47
  676.5 3.4 fusion.78
  681.2 6.4 all-gather.23
  687.6 6.6 all-gather.29
  694.2 6.9 all-gather.31
  701.2 6.9 all-gather.35
  708.2 7.0 all-gather.33
  717.9 12.0 %all-gather.30 = bf16[4,2,7200]{2,1,0:T(2,128)(2,1)S(1)} all-gather(bf16[1,2,7200]{2,1,0:T(2,128)(2,1)S(1)} %bitcast.397), channel_id=13, replica_groups=mesh['shard'=4,'replica_0'=4,'replica_1'=4,'replica_2'=2] {'replica_0'}, dimensions={0}, use_global_device_ids=true | all-gather | bytes 144000 | tf_op jit(solution)/shard_map/all_gather | solution.py:47
  729.9 13.2 %all-gather.32 = bf16[4,2,19200]{2,1,0:T(2,128)(2,1)} all-gather(bf16[1,2,19200]{2,1,0:T(2,128)(2,1)S(1)} %bitcast.392), channel_id=17, replica_groups=mesh['shard'=4,'replica_0'=4,'replica_1'=4,'replica_2'=2] {'replica_0'}, dimensions={0}, use_global_device_ids=true | all-gather | bytes 384000 | tf_op jit(solution)/shard_map/all_gather | solution.py:47
  743.0 12.7 %all-gather.12 = bf16[16,2,1,7200]{3,1,2,0:T(2,128)(2,1)S(1)} all-gather(bf16[4,2,1,7200]{3,1,2,0:T(2,128)(2,1)S(1)} %bitcast.388), channel_id=14, replica_groups=mesh['shard'=4,'replica_0'=4,'replica_1'=4,'replica_2'=2] {'replica_1'}, dimensions={0}, use_global_device_ids=true | all-gather | bytes 576000 | tf_op jit(solution)/shard_map/all_gather | solution.py:47
  758.3 12.0 %all-gather.24 = bf16[4,2,7200]{2,1,0:T(2,128)(2,1)S(1)} all-gather(bf16[1,2,7200]{2,1,0:T(2,128)(2,1)S(1)} %bitcast.396), channel_id=4, replica_groups=mesh['shard'=4,'replica_0'=4,'replica_1'=4,'replica_2'=2] {'replica_0'}, dimensions={0}, use_global_device_ids=true | all-gather | bytes 144000 | tf_op jit(solution)/shard_map/all_gather | solution.py:47
  770.3 13.1 %all-gather.36 = bf16[4,2,19200]{2,1,0:T(2,128)(2,1)} all-gather(bf16[1,2,19200]{2,1,0:T(2,128)(2,1)S(1)} %bitcast.391), channel_id=23, replica_groups=mesh['shard'=4,'replica_0'=4,'replica_1'=4,'replica_2'=2] {'replica_0'}, dimensions={0}, use_global_device_ids=true | all-gather | bytes 384000 | tf_op jit(solution)/shard_map/all_gather | solution.py:47
  783.3 12.7 %all-gather.3 = bf16[16,2,1,7200]{3,1,2,0:T(2,128)(2,1)S(1)} all-gather(bf16[4,2,1,7200]{3,1,2,0:T(2,128)(2,1)S(1)} %bitcast.389), channel_id=5, replica_groups=mesh['shard'=4,'replica_0'=4,'replica_1'=4,'replica_2'=2] {'replica_1'}, dimensions={0}, use_global_device_ids=true | all-gather | bytes 576000 | tf_op jit(solution)/shard_map/all_gather | solution.py:47
  798.6 13.2 %all-gather.34 = bf16[4,2,19200]{2,1,0:T(2,128)(2,1)} all-gather(bf16[1,2,19200]{2,1,0:T(2,128)(2,1)S(1)} %bitcast.390), channel_id=20, replica_groups=mesh['shard'=4,'replica_0'=4,'replica_1'=4,'replica_2'=2] {'replica_0'}, dimensions={0}, use_global_device_ids=true | all-gather | bytes 384000 | tf_op jit(solution)/shard_map/all_gather | solution.py:47
  814.8 6.1 fusion.89
  820.9 6.0 all-reduce.14.cloned.1.call-done
  830.7 20.4 %all-gather.47.cloned.1.call-done = bf16[16,2,1,19200]{3,1,2,0:T(2,128)(2,1)} async-done(((bf16[4,2,1,19200]{3,1,2,0:T(2,128)(2,1)}), bf16[16,2,1,19200]{3,1,2,0:T(2,128)(2,1)}) %all-gather.47.cloned.1.call-update) | async-done | bytes 1228816 | tf_op jit(solution)/shard_map/all_gather | solution.py:47
  853.2 24.7 %all-gather.51.cloned.1.call-done = bf16[16,2,1,19200]{3,1,2,0:T(2,128)(2,1)} async-done(((bf16[4,2,1,19200]{3,1,2,0:T(2,128)(2,1)}), bf16[16,2,1,19200]{3,1,2,0:T(2,128)(2,1)}) %all-gather.51.cloned.1.call-update) | async-done | bytes 1228816 | tf_op jit(solution)/shard_map/all_gather | solution.py:47
  877.8 3.6 copy_bitcast_fusion
  883.0 4.3 reshape.399
  887.3 4.0 reshape.401
  893.3 11.3 %all-gather.49.cloned.1.call-done = bf16[16,2,1,19200]{3,1,2,0:T(2,128)(2,1)} async-done(((bf16[4,2,1,19200]{3,1,2,0:T(2,128)(2,1)}), bf16[16,2,1,19200]{3,1,2,0:T(2,128)(2,1)}) %all-gather.49.cloned.1.call-update) | async-done | bytes 1228816 | tf_op jit(solution)/shard_map/all_gather | solution.py:47
  (227 shorter events, 127.2 us)
Async XLA Ops:
  7.2 3.4 copy-start.27
  7.2 3.6 copy-start.20
  7.2 3.6 copy-start.25
  7.2 56.9 %all-gather.45.cloned.1.call-start = ((), (), s32[]{:S(2)}) async-start(), calls=%async_computation.1 | async-start | bytes 6144000 | tf_op jit(solution)/shard_map/all_gather | solution.py:145
  7.9 193.7 %all-gather.43.cloned.1.call-start = ((), (), s32[]{:S(2)}) async-start(), calls=%async_computation | async-start | bytes 18739200 | tf_op jit(solution)/shard_map/all_gather | solution.py:22
  18.1 0.7 copy-start.30
  18.1 1.9 copy-start
  18.2 46.0 %copy-start.1 = (bf16[1,384,960]{1,2,0:T(8,128)(2,1)S(1)}, bf16[1,384,960]{1,2,0:T(8,128)(2,1)}, u32[]{:S(2)}) copy-start(bf16[1,384,960]{1,2,0:T(8,128)(2,1)} %param.27) | copy-start | bytes 2211844
  18.2 808.7 %all-reduce.14.cloned.1.call-start = ((), (), s32[]{:S(2)}) async-start(), calls=%async_computation.5 | async-start | bytes 1966080
  209.2 3.2 copy-start.16
  214.1 2.4 copy-start.4
  226.6 4.1 copy-start.5
  226.6 4.1 copy-start.26
  230.7 35.2 %copy-start.7 = (f32[384,960]{0,1:T(8,128)}, f32[384,960]{0,1:T(8,128)S(1)}, u32[]{:S(2)}) copy-start(f32[384,960]{0,1:T(8,128)S(1)} %get-tuple-element.266) | copy-start | bytes 4423684
  231.0 5.4 copy-start.10
  259.8 6.2 copy-start.2
  265.9 1.1 copy-start.6
  306.8 7.4 copy-start.21
  306.8 1.7 copy-start.24
  308.6 0.7 copy-start.14
  325.2 0.9 copy-start.11
  346.8 11.7 %copy-start.3 = (bf16[1,384,960]{1,2,0:T(8,128)(2,1)S(1)}, bf16[1,384,960]{1,2,0:T(8,128)(2,1)}, u32[]{:S(2)}) copy-start(bf16[1,384,960]{1,2,0:T(8,128)(2,1)} %param.27) | copy-start | bytes 2211844
  365.6 12.2 %copy-start.9 = (f32[128,2400]{1,0:T(8,128)S(1)}, f32[128,2400]{1,0:T(8,128)}, u32[]{:S(2)}) copy-start(f32[128,2400]{1,0:T(8,128)} %reshape.386) | copy-start | bytes 3686404
  600.6 70.5 %copy-start.29 = (f32[960]{0:T(1024)S(1)}, f32[960]{0:T(1024)}, u32[]{:S(2)}) copy-start(f32[960]{0:T(1024)} %get-tuple-element.194) | copy-start | bytes 11524
  600.6 70.8 %copy-start.12 = (bf16[384,15,64]{0,2,1:T(8,128)(2,1)S(1)}, bf16[384,15,64]{0,2,1:T(8,128)(2,1)}, u32[]{:S(2)}) copy-start(bf16[384,15,64]{0,2,1:T(8,128)(2,1)} %copy-done.11) | copy-start | bytes 2211844
  671.4 3.1 copy-start.18
  671.4 3.1 copy-start.15
  674.5 1.9 copy-start.22
  676.5 4.6 copy-start.23
  679.8 35.4 %copy-start.19 = (f32[4,4,2,1,2400]{4,2,1,0,3:T(2,128)S(1)}, f32[4,4,2,1,2400]{4,2,1,0,3:T(2,128)}, u32[]{:S(2)}) copy-start(f32[4,4,2,1,2400]{4,2,1,0,3:T(2,128)} %copy_bitcast_fusion.1) | copy-start | bytes 921604
  680.2 0.8 copy-start.17
  681.0 170.1 %all-gather.47.cloned.1.call-start = ((), (), s32[]{:S(2)}) async-start(), calls=%async_computation.2 | async-start | bytes 1536000 | tf_op jit(solution)/shard_map/all_gather | solution.py:47
  755.8 122.1 %all-gather.51.cloned.1.call-start = ((), (), s32[]{:S(2)}) async-start(), calls=%async_computation.4 | async-start | bytes 1536000 | tf_op jit(solution)/shard_map/all_gather | solution.py:47
  796.0 108.6 %all-gather.49.cloned.1.call-start = ((), (), s32[]{:S(2)}) async-start(), calls=%async_computation.3 | async-start | bytes 1536000 | tf_op jit(solution)/shard_map/all_gather | solution.py:47
  796.5 15.3 %copy-start.28 = (f32[384]{0:T(512)S(1)}, f32[384]{0:T(512)}, u32[]{:S(2)}) copy-start(f32[384]{0:T(512)} %get-tuple-element.261) | copy-start | bytes 4612
  811.8 3.0 copy-start.8
  811.8 3.0 copy-start.13
Sparse Core Ops, SparseCore 0:
  9.7 54.3 all-gather.44
  65.8 135.8 all-gather.42
  681.1 145.7 all-reduce.13
  828.5 22.4 all-gather.46
  852.7 25.1 all-gather.50
  879.5 25.1 all-gather.48
where the time goes:
time: 927 us; the launch traced here: 917 us
  blocking collectives  406 us (44%)
  waiting for transfers between devices  237 us (26%)
  matrix products  118 us (13%)
  local copies, waits for them, and re-layouts  114 us (12%)
  other arithmetic  26 us (3%)
  between operations  15 us (2%)
    unnamed x1, blocking collectives  223 us
    all_gather x18, blocking collectives, stacked_from(): parts = lax.all_gather(parts, axes[k])  183 us
    all_gather x1, waiting for transfers between devices, sent_together(): out, at, outs = (lax.all_gather(both, axis, axis=dim, tiled=True), 0, [])  131 us
    all_gather x3, waiting for transfers between devices, stacked_from(): parts = lax.all_gather(parts, axes[k])  56.3 us
    reshape x7, local copies, waits for them, and re-layouts, body(): m.reshape(count, -1)  53.7 us
    all_gather x1, waiting for transfers between devices, body(): lax.all_gather(pieces[8], 'shard', axis=0, tiled=True)  43 us
    dot_general x7, matrix products, mult_nt(): lax.dot_general(left, right, (((1,), (1,)), ((), ())), preferred_element_...  29.8 us
    dot_general x7, matrix products, mult(): return jnp.dot(left, right, preferred_element_type=jnp.float32)  28.9 us
  transfers between devices with their start and end apart: 6, of which 6 were waited for; matrix products, arithmetic and copies ran while one was open for 6% of the time, Pallas kernels for 0%

commit v1 on v0

v1 whole, which is shorter than its diff:
```python
import jax
import jax.numpy as jnp
from jax import lax
from jax.experimental import pallas as pl
from jax.experimental.pallas import tpu as pltpu
from jax.sharding import Mesh
from jax.sharding import PartitionSpec as P

T = 384
D = 960
FF = 2560
HEADS = 15
KV = 5
GROUP = 3
HEAD_DIM = 64
BLOCK = 128
BLOCKS = T // BLOCK
STACK = GROUP * BLOCK
QK = (HEADS + KV) * HEAD_DIM
QKV = QK + KV * HEAD_DIM
AT_QKV = 1024
PACK = AT_QKV + QKV
ROWS = D // 4
TOP = 128
UNIT = 640
EVERY = ("y_lo", "core", "z", "x", "y_hi")
SHARD = ("y_lo", "core")
EPS = 1e-05
BASE = 100000.0
MASKED = -1e30
BF = jnp.bfloat16
F32 = jnp.float32
LIMIT = 52 * 2**20

ANY = pl.BlockSpec(memory_space=pl.ANY)
VMEM = pl.BlockSpec(memory_space=pltpu.VMEM)
SMEM = pl.BlockSpec(memory_space=pltpu.SMEM)


def shape(*dims, dtype=BF):
    return jax.ShapeDtypeStruct(dims, dtype)


def mult(left, right):
    return jnp.dot(left, right, preferred_element_type=F32)


def mult_tn(left, right):
    return lax.dot_general(left, right, (((0,), (0,)), ((), ())), preferred_element_type=F32)


def mult_nt(left, right):
    return lax.dot_general(left, right, (((1,), (1,)), ((), ())), preferred_element_type=F32)


def piece_copies(pieces, full, me, rows, top, sems, columns=None):
    copies = []
    for k, (flip, start, size) in enumerate(
        ((0, 0, rows), (1, 0, rows), (2, 0, top), (2, top, rows - top), (3, 0, top), (3, top, rows - top))
    ):
        at = pl.multiple_of(lax.bitwise_xor(me, jnp.int32(flip)) * rows + start, 16)
        source, target = pieces[k], full.at[pl.ds(at, size)]
        if columns is not None:
            source, target = source.at[:, columns], full.at[pl.ds(at, size), columns]
        copies.append(pltpu.make_async_copy(source, target, sems.at[k]))
    return copies


def rope(u, cosine, sine, sign):
    lane = lax.broadcasted_iota(jnp.int32, u.shape, 1)
    turned = jnp.where(lane % HEAD_DIM < HEAD_DIM // 2, pltpu.roll(u, 96, 1), pltpu.roll(u, 32, 1))
    return u * cosine + sign * (turned * sine)


def rms_scale(v):
    return lax.rsqrt(jnp.mean(v * v, axis=-1, keepdims=True) + EPS)


def norm_back(v, gain, grad):
    scale = rms_scale(v)
    inner = grad * gain
    d_v = scale * inner - v * (scale * scale * scale) * jnp.mean(v * inner, axis=-1, keepdims=True)
    return d_v, jnp.sum(grad * v * scale, axis=0, keepdims=True)


def attention_kernel(me_ref, x_ref, gains_ref, cos_ref, sin_ref, start_ref, *refs):
    pieces, refs = refs[:6], refs[6:]
    (a_ref, q_ref, k_ref, v_ref, p0_ref, p1_ref, p2_ref, att_ref, h_ref, b_ref, w, o, bias, sems) = refs
    copies = piece_copies(pieces, w, me_ref[0], ROWS, TOP, sems)
    for copy in copies:
        copy.start()
    x = x_ref[...].astype(F32)
    a_ref[...] = (x * rms_scale(x) * gains_ref[0:1]).astype(BF)
    column = lax.broadcasted_iota(jnp.int32, (T, T), 1)
    row = lax.broadcasted_iota(jnp.int32, (T, T), 0)
    bias[...] = jnp.where((column >= start_ref[...]) & (column <= row), 0.0, MASKED)
    for copy in copies:
        copy.wait()
    a = a_ref[...]
    for c in range(QK // 256):
        wide = mult(a, w[:, AT_QKV + 256 * c : AT_QKV + 256 * (c + 1)])
        for half in range(2):
            u = rope(wide[:, 128 * half : 128 * half + 128], cos_ref[...], sin_ref[...], 1.0).astype(BF)
            for side in range(2):
                head = 4 * c + 2 * half + side
                one = u[:, HEAD_DIM * side : HEAD_DIM * (side + 1)]
                if head < HEADS:
                    for i in range(BLOCKS):
                        at = i * STACK + head % GROUP * BLOCK
                        q_ref[head // GROUP, at : at + BLOCK, :] = one[i * BLOCK : (i + 1) * BLOCK]
                else:
                    k_ref[head - HEADS] = one
    values = mult(a, w[:, AT_QKV + QK :]).astype(BF)
    for j in range(KV):
        v_ref[j] = values[:, HEAD_DIM * j : HEAD_DIM * (j + 1)]
    probs = (p0_ref, p1_ref, p2_ref)

    def one_group(j, carry):
        for i in range(BLOCKS):
            keys = (i + 1) * BLOCK
            q = q_ref[j, i * STACK : (i + 1) * STACK, :]
            scores = mult_nt(q, k_ref[j, :keys, :]) * 0.125
            part = bias[i * BLOCK : (i + 1) * BLOCK, :keys]
            scores = scores + jnp.concatenate([part] * GROUP, axis=0)
            expo = jnp.exp(scores - jnp.max(scores, axis=-1, keepdims=True))
            prob = (expo * (1.0 / jnp.sum(expo, axis=-1, keepdims=True))).astype(BF)
            probs[i][j] = prob
            o[j, i * STACK : (i + 1) * STACK, :] = mult(prob, v_ref[j, :keys, :])
        return carry

    lax.fori_loop(0, KV, one_group, 0)
    for c in range(8):
        heads = [stacked_head(o, head) for head in range(2 * c, min(2 * c + 2, HEADS))]
        wide = jnp.concatenate(heads, axis=1) if len(heads) > 1 else heads[0]
        att_ref[:, 128 * c : 128 * c + wide.shape[1]] = wide.astype(BF)
    h = x_ref[...].astype(F32) + mult(att_ref[...], w[:, :D])
    h_ref[...] = h
    b_ref[...] = (h * rms_scale(h) * gains_ref[1:2]).astype(BF)


def stacked_head(ref, head):
    at = head % GROUP * BLOCK
    return jnp.concatenate(
        [ref[head // GROUP, i * STACK + at : i * STACK + at + BLOCK, :] for i in range(BLOCKS)], axis=0
    )


CHUNK = 512


def gate_kernel(me_ref, b_ref, *refs):
    pieces, (act_ref, silu_ref, slope_ref, w, sems) = refs[:6], refs[6:]
    chunks = FF // CHUNK
    copies = []
    for c in range(chunks):
        for k in range(2):
            columns = pl.ds(k * FF + c * CHUNK, CHUNK)
            copies.append(piece_copies(pieces, w, me_ref[0], ROWS, TOP, sems.at[2 * c + k], columns))
    for group in copies:
        for copy in group:
            copy.start()
    b = b_ref[...]
    for c in range(chunks):
        at = c * CHUNK
        for group in copies[2 * c : 2 * c + 2]:
            for copy in group:
                copy.wait()
        gate = mult(b, w[:, at : at + CHUNK])
        up = mult(b, w[:, FF + at : FF + at + CHUNK])
        sigma = jax.nn.sigmoid(gate)
        silu = gate * sigma
        act_ref[:, at : at + CHUNK] = (silu * up).astype(BF)
        silu_ref[:, at : at + CHUNK] = silu.astype(BF)
        slope_ref[:, at : at + CHUNK] = (up * sigma * (1.0 + gate * (1.0 - sigma))).astype(BF)


def mlp_kernel(me_ref, act_ref, silu_ref, slope_ref, h_ref, dy_ref, gains_ref, *refs):
    down, wide, refs = refs[:6], refs[6:12], refs[12:]
    (out_ref, d_gate_ref, d_up_ref, d_h_ref, d_low_ref, d_gain_ref, wd, w, sums, sems) = refs
    first = piece_copies(down, wd, me_ref[0], FF // 4, FF // 8, sems.at[0])
    second = piece_copies(wide, w, me_ref[0], ROWS, TOP, sems.at[1])
    for copy in first + second:
        copy.start()
    for copy in first:
        copy.wait()
    dy = dy_ref[...]
    out_ref[...] = (h_ref[...] + mult(act_ref[...], wd[...])).astype(BF)
    for c in range(FF // CHUNK):
        at = c * CHUNK
        d_act = mult_nt(dy, wd[at : at + CHUNK, :])
        d_gate_ref[:, at : at + CHUNK] = (d_act * slope_ref[:, at : at + CHUNK].astype(F32)).astype(BF)
        d_up_ref[:, at : at + CHUNK] = (d_act * silu_ref[:, at : at + CHUNK].astype(F32)).astype(BF)
    for copy in second:
        copy.wait()
    sums[...] = mult_nt(d_gate_ref[...], w[:, :FF]) + mult_nt(d_up_ref[...], w[:, FF:])
    d_norm, d_gain = norm_back(h_ref[...], gains_ref[1:2], sums[...])
    d_h = dy.astype(F32) + d_norm
    d_h_ref[...] = d_h
    d_low_ref[...] = d_h.astype(BF)
    d_gain_ref[...] = d_gain


def attention_back_kernel(me_ref, x_ref, gains_ref, cos_ref, sin_ref, d_low_ref, d_h_ref, q_ref, k_ref, v_ref, p0_ref, p1_ref, p2_ref, *refs):
    pieces, refs = refs[:6], refs[6:]
    (d_qkv_ref, grad_ref, d_gain_ref, w, d_o, d_q, d_k, d_v, sems) = refs
    copies = piece_copies(pieces, w, me_ref[0], ROWS, TOP, sems)
    for copy in copies:
        copy.start()
    for copy in copies:
        copy.wait()
    d_low = d_low_ref[...]
    for c in range(3):
        part = mult_nt(d_low, w[320 * c : 320 * (c + 1), :D]).astype(BF)
        for side in range(5):
            head = 5 * c + side
            for i in range(BLOCKS):
                at = i * STACK + head % GROUP * BLOCK
                d_o[head // GROUP, at : at + BLOCK, :] = part[i * BLOCK : (i + 1) * BLOCK, HEAD_DIM * side : HEAD_DIM * (side + 1)]
    probs = (p0_ref, p1_ref, p2_ref)

    def one_group(j, carry):
        parts_k, parts_v = [], []
        for i in range(BLOCKS):
            keys = (i + 1) * BLOCK
            stack = slice(i * STACK, (i + 1) * STACK)
            low = probs[i][j]
            d_one = d_o[j, stack, :]
            prob = low.astype(F32)
            d_prob = mult_nt(d_one, v_ref[j, :keys, :])
            inner = jnp.sum(prob * d_prob, axis=-1, keepdims=True)
            d_scores = (prob * (d_prob - inner)).astype(BF)
            d_q[j, stack, :] = mult(d_scores, k_ref[j, :keys, :]) * 0.125
            parts_k.append(mult_tn(d_scores, q_ref[j, stack, :]))
            parts_v.append(mult_tn(low, d_one))
        for i in range(BLOCKS):
            rows = slice(i * BLOCK, (i + 1) * BLOCK)
            d_k[j, rows, :] = sum(part[rows] for part in parts_k[i:]) * 0.125
            d_v[j, rows, :] = sum(part[rows] for part in parts_v[i:])
        return carry

    lax.fori_loop(0, KV, one_group, 0)
    for c in range(QK // 128):
        heads = []
        for head in (2 * c, 2 * c + 1):
            heads.append(stacked_head(d_q, head) if head < HEADS else d_k[head - HEADS])
        u = jnp.concatenate(heads, axis=1)
        d_qkv_ref[:, 128 * c : 128 * (c + 1)] = rope(u, cos_ref[...], sin_ref[...], -1.0).astype(BF)
    for c in range(3):
        heads = [d_v[j] for j in range(2 * c, min(2 * c + 2, KV))]
        wide = jnp.concatenate(heads, axis=1) if len(heads) > 1 else heads[0]
        d_qkv_ref[:, QK + 128 * c : QK + 128 * c + wide.shape[1]] = wide.astype(BF)
    d_a = mult_nt(d_qkv_ref[...], w[:, AT_QKV:])
    d_norm, d_gain = norm_back(x_ref[...].astype(F32), gains_ref[0:1], d_a)
    grad_ref[...] = d_h_ref[...] + d_norm
    d_gain_ref[...] = d_gain


FLIPS = (3, 2, 1, 0)


def down_grad_kernel(me_ref, act_ref, dy_ref, *outs):
    dy = dy_ref[...]
    for flip, out in zip(FLIPS, outs):
        at = pl.multiple_of(lax.bitwise_xor(me_ref[0], jnp.int32(flip)) * (FF // 4), 128)
        out[...] = mult_tn(act_ref[:, pl.ds(at, FF // 4)], dy).astype(BF)


def wide_grad_kernel(me_ref, b_ref, d_gate_ref, d_up_ref, *refs):
    outs, (full,) = refs[:4], refs[4:]
    for c in range(4):
        for k, source in enumerate((d_gate_ref, d_up_ref)):
            full[2 * c + k] = mult(b_ref[...], source[:, UNIT * c : UNIT * (c + 1)]).astype(BF)
            for flip, out in zip(FLIPS, outs):
                at = pl.multiple_of(lax.bitwise_xor(me_ref[0], jnp.int32(flip)) * ROWS, 16)
                out[c, ROWS * k : ROWS * (k + 1), :] = full[2 * c + k, pl.ds(at, ROWS), :]


def attention_grad_kernel(me_ref, a_ref, att_ref, d_qkv_ref, d_low_ref, gain_ref, *refs):
    outs, (full,) = refs[:4], refs[4:]
    a, att = a_ref[...], att_ref[...]
    full[0] = mult(a, d_qkv_ref[:, :UNIT]).astype(BF)
    full[1] = mult(a, d_qkv_ref[:, UNIT : 2 * UNIT]).astype(BF)
    full[2] = jnp.concatenate([mult(a, d_qkv_ref[:, 2 * UNIT :]), mult(att, d_low_ref[:, : UNIT // 2])], axis=1).astype(BF)
    full[3] = mult(att, d_low_ref[:, UNIT // 2 :]).astype(BF)
    for flip, out in zip(FLIPS, outs):
        place = lax.bitwise_xor(me_ref[0], jnp.int32(flip))
        at = pl.multiple_of(place * ROWS, 16)
        for c in range(4):
            out[c, :ROWS, :] = full[c, pl.ds(at, ROWS), :]
            out[c, ROWS:, :] = gain_ref[place] if c == 0 else jnp.zeros((16, UNIT), BF)


def final_kernel(place_ref, *refs):
    down, wide, first = refs[:4], refs[4:8], refs[8:12]
    (query_ref, key_ref, value_ref, proj_ref, gain_ref, gate_ref, up_ref, down_ref, full) = refs[12:]
    for k, by in enumerate((0, 3, 1, 2)):
        z = lax.rem(place_ref[0] + by, 4)
        x = lax.rem(place_ref[1] + by, 4)
        down_ref[pl.ds(pl.multiple_of(z * (FF // 16), 16), FF // 16), :] = down[k][...].astype(F32)
        columns = pl.ds(pl.multiple_of(x * UNIT, 128), UNIT)
        gate_ref[:, columns] = wide[k][:ROWS].astype(F32)
        up_ref[:, columns] = wide[k][ROWS:].astype(F32)
        full[:, pl.ds(pl.multiple_of(z * UNIT, 128), UNIT)] = first[k][...].astype(F32)
    query_ref[...] = full[:ROWS, :D]
    key_ref[...] = full[:ROWS, D:QK]
    value_ref[...] = full[:ROWS, QK:QKV]
    proj_ref[...] = full[:ROWS, QKV:]
    gain_ref[...] = full[ROWS : ROWS + 8, :256]


def run(kernel, name, ins, specs, outs, scratch, flops, out_specs=None):
    moved = sum(a.size * a.dtype.itemsize for a in ins) + sum(o.size * o.dtype.itemsize for o in outs)
    return pl.pallas_call(
        kernel,
        name=name,
        out_shape=outs,
        in_specs=specs,
        out_specs=out_specs or [VMEM] * len(outs),
        scratch_shapes=scratch,
        cost_estimate=pl.CostEstimate(flops=flops, bytes_accessed=moved, transcendentals=0),
        compiler_params=pltpu.CompilerParams(vmem_limit_bytes=LIMIT),
    )(*ins)


def swap_cores(value):
    return lax.ppermute(value, "core", [(0, 1), (1, 0)])


def shift_ring(value, axis, by):
    return lax.ppermute(value, axis, [(i, (i + by) % 4) for i in range(4)])


def shift_y(value, by):
    place = [(y % 2) * 2 + y // 2 for y in range(4)]
    return lax.ppermute(value, ("y_lo", "y_hi"), [(place[y], place[(y + by) % 4]) for y in range(4)])


def gathered(shard, top):
    near = swap_cores(shard)
    far = (shift_y(shard[:top], 1), shift_y(shard[top:], -1))
    return [shard, near, *far, swap_cores(far[0]), swap_cores(far[1])]


def in_order(parts, low, core):
    parts = jnp.where(core == 1, parts[jnp.array([1, 0, 3, 2])], parts)
    return jnp.where(low == 1, parts[jnp.array([2, 3, 0, 1])], parts)


def add_low(*terms):
    total = terms[0].astype(F32)
    for term in terms[1:]:
        total = total + term.astype(F32)
    return total.astype(BF)


def piece_of(value, axis, by):
    place = lax.rem(lax.axis_index(axis) + by, 4)
    return lax.dynamic_index_in_dim(value, place, 0, keepdims=False)


def ring_scatter(value, axis):
    got = [shift_ring(piece_of(value, axis, by % 4), axis, by) for by in (1, -1, 2)]
    return add_low(piece_of(value, axis, 0), *got)


def ring_gather(value, axis):
    return [value] + [shift_ring(value, axis, by) for by in (1, -1, 2)]


def ring_joined(value, axis):
    pieces = ring_gather(value, axis)
    out = jnp.zeros((4, *value.shape), value.dtype)
    place = lax.axis_index(axis)
    for by, piece in zip((0, 3, 1, 2), pieces):
        out = lax.dynamic_update_index_in_dim(out, piece, lax.rem(place + by, 4), 0)
    return out.reshape(4 * value.shape[0], *value.shape[1:])


def chip_pair(blocks):
    theirs = add_low(blocks[1], swap_cores(blocks[0]))
    mine = swap_cores(blocks[2])
    top, bottom = shift_y(theirs[:2], 1), shift_y(theirs[2:], -1)
    return add_low(blocks[3], mine, jnp.concatenate([top, bottom]))


def scattered(blocks, first, second):
    part = ring_scatter(chip_pair(blocks), first)
    part = ring_scatter(part.reshape(4, part.shape[0] // 4, part.shape[1]), second)
    return add_low(part, lax.ppermute(part, "y_hi", [(0, 1), (1, 0)]))


def body(tokens, lengths, norm_attn, w_query, w_key, w_value, w_out, norm_mlp, w_gate, w_up, w_down, cotangent):
    low, core = lax.axis_index("y_lo"), lax.axis_index("core")
    me = (low * 2 + core).astype(jnp.int32)[None]
    pad = jnp.zeros((ROWS, AT_QKV - D), BF)
    first = gathered(jnp.concatenate([w_out, pad, w_query, w_key, w_value], axis=1), TOP)
    own = jnp.stack([norm_attn, norm_mlp])
    pair = jnp.stack([own, shift_y(own, 1)])
    other = swap_cores(pair)
    gains = in_order(jnp.stack([pair[0], other[0], pair[1], other[1]]), low, core)
    gains = gains.transpose(1, 0, 2).reshape(2, D).astype(F32)
    wide = gathered(jnp.concatenate([w_gate, w_up], axis=1), TOP)
    down = gathered(w_down, FF // 8)

    x, dy = tokens[0], cotangent[0]
    slots = jnp.arange(T, dtype=jnp.int32)
    ends = jnp.cumsum(lengths[0])
    start = jnp.max(jnp.where(slots[:, None] >= ends[None, :], ends[None, :], 0), axis=1)
    freq = BASE ** (-jnp.arange(HEAD_DIM // 2, dtype=F32) * 2.0 / HEAD_DIM)
    angle = (slots - start).astype(F32)[:, None] * freq[None, :]
    cosine = jnp.tile(jnp.cos(angle), (1, 4))
    sine = jnp.sin(angle)
    sine = jnp.tile(jnp.concatenate([-sine, sine], axis=1), (1, 2))
    start = start[:, None]

    dma = pltpu.SemaphoreType.DMA
    a_low, q, k, v, p0, p1, p2, att, h, b_low = run(
        attention_kernel,
        "attention",
        (me, x, gains, cosine, sine, start, *first),
        [SMEM] + [VMEM] * 5 + [ANY] * 6,
        [
            shape(T, D),
            shape(KV, GROUP * T, HEAD_DIM),
            shape(KV, T, HEAD_DIM),
            shape(KV, T, HEAD_DIM),
            *(shape(KV, STACK, BLOCK * (i + 1)) for i in range(BLOCKS)),
            shape(T, D),
            shape(T, D, dtype=F32),
            shape(T, D),
        ],
        [pltpu.VMEM((D, PACK), BF), pltpu.VMEM((KV, GROUP * T, HEAD_DIM), F32), pltpu.VMEM((T, T), F32), dma((6,))],
        2 * T * D * 2560 + 4 * HEADS * T * T * 128,
    )
    act, silu, slope = run(
        gate_kernel,
        "gate_up",
        (me, b_low, *wide),
        [SMEM, VMEM] + [ANY] * 6,
        [shape(T, FF)] * 3,
        [pltpu.VMEM((D, 2 * FF), BF), dma((2 * FF // CHUNK, 6))],
        4 * T * D * FF,
    )
    down_blocks = run(
        down_grad_kernel,
        "down_grad",
        (me, act, dy),
        [SMEM, VMEM, VMEM],
        [shape(FF // 4, D)] * 4,
        [],
        2 * T * D * FF,
    )
    result, d_gate, d_up, d_h, d_low, d_gain_mlp = run(
        mlp_kernel,
        "mlp_back",
        (me, act, silu, slope, h, dy, gains, *down, *wide),
        [SMEM] + [VMEM] * 6 + [ANY] * 12,
        [shape(T, D), shape(T, FF), shape(T, FF), shape(T, D, dtype=F32), shape(T, D), shape(1, D, dtype=F32)],
        [pltpu.VMEM((FF, D), BF), pltpu.VMEM((D, 2 * FF), BF), pltpu.VMEM((T, D), F32), dma((2, 6))],
        8 * T * D * FF,
    )
    down_part = scattered([b.reshape(4, FF // 16, D) for b in down_blocks], "z", "x")
    wide_blocks = run(
        wide_grad_kernel,
        "gate_up_grad",
        (me, b_low.T, d_gate, d_up),
        [SMEM] + [VMEM] * 3,
        [shape(4, 2 * ROWS, UNIT)] * 4,
        [pltpu.VMEM((8, D, UNIT), BF)],
        4 * T * D * FF,
    )
    wide_part = scattered(wide_blocks, "x", "z")
    d_qkv, grad_input, d_gain_attn = run(
        attention_back_kernel,
        "attention_back",
        (me, x, gains, cosine, sine, d_low, d_h, q, k, v, p0, p1, p2, *first),
        [SMEM] + [VMEM] * 12 + [ANY] * 6,
        [shape(T, QKV), shape(T, D, dtype=F32), shape(1, D, dtype=F32)],
        [
            pltpu.VMEM((D, PACK), BF),
            pltpu.VMEM((KV, GROUP * T, HEAD_DIM), BF),
            pltpu.VMEM((KV, GROUP * T, HEAD_DIM), F32),
            pltpu.VMEM((KV, T, HEAD_DIM), F32),
            pltpu.VMEM((KV, T, HEAD_DIM), F32),
            dma((6,)),
        ],
        2 * T * D * 2560 + 8 * HEADS * T * T * 128,
    )
    d_gains = jnp.concatenate([d_gain_attn, d_gain_mlp]).reshape(2, 4, ROWS).transpose(1, 0, 2)
    d_gains = jnp.pad(d_gains, ((0, 0), (0, 14), (0, UNIT - ROWS))).astype(BF)
    first_blocks = run(
        attention_grad_kernel,
        "attention_grad",
        (me, a_low.T, att.T, d_qkv, d_low, d_gains),
        [SMEM] + [VMEM] * 5,
        [shape(4, ROWS + 16, UNIT)] * 4,
        [pltpu.VMEM((4, D, UNIT), BF)],
        2 * T * D * FF,
    )
    first_part = scattered(first_blocks, "z", "x")
    down_all = ring_gather(ring_joined(down_part, "x"), "z")
    wide_all = ring_gather(ring_joined(wide_part, "z"), "x")
    first_all = ring_gather(ring_joined(first_part, "x"), "z")
    place = jnp.stack([lax.axis_index("z"), lax.axis_index("x")]).astype(jnp.int32)
    query, key, value, proj, gain, gate, up, down_grad = run(
        final_kernel,
        "place_gradients",
        (place, *down_all, *wide_all, *first_all),
        [SMEM] + [VMEM] * 12,
        [
            shape(ROWS, D, dtype=F32),
            shape(ROWS, KV * HEAD_DIM, dtype=F32),
            shape(ROWS, KV * HEAD_DIM, dtype=F32),
            shape(ROWS, D, dtype=F32),
            shape(8, 256, dtype=F32),
            shape(ROWS, FF, dtype=F32),
            shape(ROWS, FF, dtype=F32),
            shape(FF // 4, D, dtype=F32),
        ],
        [pltpu.VMEM((ROWS + 16, FF), F32)],
        0,
    )
    return (result[None], grad_input[None], gain[0, :ROWS], query, key, value, proj, gain[1, :ROWS], gate, up, down_grad)


def solution(mesh):
    torus = Mesh(mesh.devices.reshape(2, 2, 4, 4, 2), EVERY)
    rows = P(EVERY, None, None)
    weight = P(SHARD, None)
    gain = P(SHARD)
    return jax.shard_map(
        body,
        mesh=torus,
        in_specs=(rows, P(EVERY, None), gain, weight, weight, weight, weight, gain, weight, weight, weight, rows),
        out_specs=(rows, rows, gain, weight, weight, weight, weight, gain, weight, weight, weight),
        check_vma=False,
    )
```

time: 927 us -> 400 us (0.43)
  the two profiles are of different devices: /device:TPU:0 before, /device:TPU:8 now
where the time goes in v1:
time: 400 us; the launch traced here: 392 us
  waiting for transfers between devices  141 us (35%)
  starting transfers between devices  99.4 us (25%)
  Pallas kernels  92.7 us (23%)
  local copies, waits for them, and re-layouts  46.1 us (12%)
  other arithmetic  11.8 us (3%)
    pallas_call x8, Pallas kernels, run(): pl.pallas_call(kernel, name=name, out_shape=outs, in_specs=specs, out_spe...  92.7 us
    ppermute x36, starting transfers between devices, shift_ring(): return lax.ppermute(value, axis, [(i, (i + by) % 4) for i in range(4)])  69.4 us
    ppermute x13, waiting for transfers between devices, shift_y(): lax.ppermute(value, ('y_lo', 'y_hi'), [(place[y], place[(y + by) % 4]) fo...  60.8 us
    ppermute x36, waiting for transfers between devices, shift_ring(): return lax.ppermute(value, axis, [(i, (i + by) % 4) for i in range(4)])  60.1 us
    ppermute x3, waiting for transfers between devices, scattered(): return add_low(part, lax.ppermute(part, 'y_hi', [(0, 1), (1, 0)]))  19.9 us
    unnamed x59, local copies, waits for them, and re-layouts  18.6 us
    ppermute x13, starting transfers between devices, shift_y(): lax.ppermute(value, ('y_lo', 'y_hi'), [(place[y], place[(y + by) % 4]) fo...  18.3 us
    convert_element_type x12, other arithmetic, add_low(): return total.astype(BF)  10.9 us
  transfers between devices with their start and end apart: 68, of which 24 were waited for; matrix products, arithmetic and copies ran while one was open for 12% of the time, Pallas kernels for 22%

profile of v1, /device:TPU:8, one launch (start us, length us, event | category | flops | bytes accessed | tf_op | source)
XLA Modules:
  0.0 392.3 jit_solution(17483804745617190856)
XLA Ops:
  5.8 2.3 concatenate.23.refs_0_
  16.6 2.3 slice.73
  19.0 2.8 collective-permute-start.9
  21.9 2.5 slice.72
  26.3 3.2 collective-permute-done.13.refs_2_
  29.5 2.5 collective-permute-start.3
  32.0 7.9 %collective-permute-done.14.refs_3_ = bf16[320,960]{1,0:T(8,128)(2,1)} collective-permute-done((bf16[320,960]{1,0:T(8,128)(2,1)S(1)}, bf16[320,960]{1,0:T(8,128)(2,1)}, u32[]{:S(2)}, u32[]{:S(2)}) %collective-permute-start.14) | collective-permute-done | bytes 614432 | tf_op jit(solution)/shard_map/ppermute | solution.py:335
  40.2 30.9 %collective-permute-done.3 = bf16[128,2624]{0,1:T(8,128)(2,1)} collective-permute-done((bf16[128,2624]{0,1:T(8,128)(2,1)S(1)}, bf16[128,2624]{0,1:T(8,128)(2,1)}, u32[]{:S(2)}, u32[]{:S(2)}) %collective-permute-start.3) | collective-permute-done | bytes 671776 | tf_op jit(solution)/shard_map/ppermute | solution.py:335
  79.4 2.5 copy.108.refs_1_
  84.9 15.8 %attention.1 = (bf16[384,960]{1,0:T(8,128)(2,1)}, bf16[5,1152,64]{2,1,0:T(8,128)(2,1)}, bf16[5,384,64]{2,1,0:T(8,128)(2,1)S(1)}, bf16[5,384,64]{2,1,0:T(8,128)(2...) custom-call(s32[1]{0:T(128)} %bitcast.me_ref, ...), custom_call_target="tpu_custom_call" | custom-call | flops 3019898880 | bytes 14042116 | tf_op jit(solution)/shard_map/attention/pallas_call | solution.py:313
  105.4 10.0 %gate_up.1 = (bf16[384,2560]{1,0:T(8,128)(2,1)}, bf16[384,2560]{1,0:T(8,128)(2,1)}, bf16[384,2560]{1,0:T(8,128)(2,1)}) custom-call(s32[1]{0:T(128)} %bitcast.me_ref, bf16[384,960]{1,0:T(8,128)(2,1)S(1)} %copy-done.1, bf16[240,5120]{1,0:T(8,128)(2,1)} %constant_dynamic-update-slice_fusion.refs_0_.refs_6_, ...), custom_call_target="tpu_custom_call" | custom-call | flops 3774873600 | bytes 16465924 | tf_op jit(solution)/shard_map/gate_up/pallas_call | solution.py:313
  115.5 5.5 %down_grad.1 = (bf16[640,960]{1,0:T(8,128)(2,1)}, bf16[640,960]{1,0:T(8,128)(2,1)}, bf16[640,960]{1,0:T(8,128)(2,1)}, bf16[640,960]{1,0:T(8,128)(2,1)}) custom-call(s32[1]{0:T(128)} %bitcast.me_ref, bf16[384,2560]{1,0:T(8,128)(2,1)} %get-tuple-element.54.act_ref, bf16[384,960]{1,0:T(8,128)(2,1)S(1)} %bitcast.122), custom_call_target="tpu_custom_call" | custom-call | flops 1887436800 | bytes 7618564 | tf_op jit(solution)/shard_map/down_grad/pallas_call | solution.py:313
  122.0 16.6 %mlp_back.1 = (bf16[384,960]{1,0:T(8,128)(2,1)}, bf16[384,2560]{1,0:T(8,128)(2,1)}, bf16[384,2560]{1,0:T(8,128)(2,1)}, f32[384,960]{1,0:T(8,128)}, bf16[384,960]{1,0:T(8,128)(2,1)}, /*index=5*/f32[1,960]{1,0:T(1,128)S(1)}) custom-call(s32[1]{0:T(128)} %bitcast.me_ref, bf16[384,2560]{1,0:T(8,128)(2,1)} %get-tuple-element.54.act_ref, ...), custom_call_target="tpu_custom_call" | custom-call | flops 7549747200 | bytes 29748484 | tf_op jit(solution)/shard_map/mlp_back/pallas_call | solution.py:313
  138.6 19.2 %attention_back.1 = (bf16[384,1600]{1,0:T(8,128)(2,1)}, f32[384,960]{1,0:T(8,128)}, f32[1,960]{1,0:T(1,128)S(1)}) custom-call(s32[1]{0:T(128)} %bitcast.me_ref, bf16[384,960]{1,0:T(8,128)(2,1)} %bitcast.142, f32[2,960]{1,0:T(2,128)S(1)} %reshape.153.gains_ref, f32[384,128]{1,0:T(8,128)S(1)} %copy.99.cos_ref, f32[384,128]{1,0:T(8,128)S(1)} %copy.100.sin_ref, ...), custom_call_target="tpu_custom_call" | custom-call | flops 4152360960 | bytes 15273220 | tf_op jit(solution)/shard_map/attention_back/pallas_call | solution.py:313
  157.9 7.1 %attention_grad.1 = (bf16[4,256,640]{2,1,0:T(8,128)(2,1)}, bf16[4,256,640]{2,1,0:T(8,128)(2,1)}, bf16[4,256,640]{2,1,0:T(8,128)(2,1)}, bf16[4,256,640]{2,1,0:T(8,128)(2,1)}) custom-call(s32[1]{0:T(128)} %bitcast.me_ref, bf16[960,384]{1,0:T(8,128)(2,1)S(1)} %bitcast.124, bf16[960,384]{1,0:T(8,128)(2,1)S(1)} %bitcast.125, ...), custom_call_target="tpu_custom_call" | custom-call | flops 1887436800 | bytes 8765444 | tf_op jit(solution)/shard_map/attention_grad/pallas_call | solution.py:313
  166.3 12.1 %gate_up_grad.1 = (bf16[4,480,640]{2,1,0:T(8,128)(2,1)}, bf16[4,480,640]{2,1,0:T(8,128)(2,1)}, bf16[4,480,640]{2,1,0:T(8,128)(2,1)}, bf16[4,480,640]{2,1,0:T(8,128)(2,1)}) custom-call(s32[1]{0:T(128)} %bitcast.me_ref, bf16[960,384]{1,0:T(8,128)(2,1)S(1)} %bitcast.126, bf16[384,2560]{1,0:T(8,128)(2,1)} %get-tuple-element.72.d_gate_ref, ...), custom_call_target="tpu_custom_call" | custom-call | flops 3774873600 | bytes 14499844 | tf_op jit(solution)/shard_map/gate_up_grad/pallas_call | solution.py:313
  188.1 12.1 %collective-permute-done.19 = bf16[2,160,960]{2,1,0:T(8,128)(2,1)} collective-permute-done((bf16[2,160,960]{2,1,0:T(8,128)(2,1)S(1)}, bf16[2,160,960]{2,1,0:T(8,128)(2,1)}, u32[]{:S(2)}, u32[]{:S(2)}) %collective-permute-start.19) | collective-permute-done | bytes 614432 | tf_op jit(solution)/shard_map/ppermute | solution.py:335
  200.2 3.3 collective-permute-start.54
  203.5 2.9 fusion.2
  208.5 5.1 %collective-permute-done.53 = bf16[2,256,640]{2,1,0:T(8,128)(2,1)S(1)} collective-permute-done((bf16[2,256,640]{2,1,0:T(8,128)(2,1)}, bf16[2,256,640]{2,1,0:T(8,128)(2,1)S(1)}, u32[]{:S(2)}, u32[]{:S(2)}) %collective-permute-start.53) | collective-permute-done | bytes 655392 | tf_op jit(solution)/shard_map/ppermute | solution.py:335
  213.6 4.0 %collective-permute-start.22 = (bf16[160,960]{1,0:T(8,128)(2,1)S(1)}, bf16[160,960]{1,0:T(8,128)(2,1)S(1)}, u32[]{:S(2)}, u32[]{:S(2)}) collective-permute-start(bf16[160,960]{1,0:T(8,128)(2,1)S(1)} %get-tuple-element.157), channel_id=1, source_target_pairs={{0,24},{8,0},{16,8},{24,16},{1,25},{9,1},{17,9},{25,17},{2,26},{10... | collective-permute-start | bytes 921608 | tf_op jit(solution)/shard_map/ppermute | solution.py:330
  217.6 2.6 collective-permute-start.23
  223.4 8.0 %collective-permute-done.22 = bf16[160,960]{1,0:T(8,128)(2,1)S(1)} collective-permute-done((bf16[160,960]{1,0:T(8,128)(2,1)S(1)}, bf16[160,960]{1,0:T(8,128)(2,1)S(1)}, u32[]{:S(2)}, u32[]{:S(2)}) %collective-permute-start.22) | collective-permute-done | bytes 307232 | tf_op jit(solution)/shard_map/ppermute | solution.py:330
  231.5 4.1 %collective-permute-start.56 = (bf16[256,640]{1,0:T(8,128)(2,1)S(1)}, bf16[256,640]{1,0:T(8,128)(2,1)S(1)}, u32[]{:S(2)}, u32[]{:S(2)}) collective-permute-start(bf16[256,640]{1,0:T(8,128)(2,1)S(1)} %get-tuple-element.152), channel_id=1, source_target_pairs={{0,24},{8,0},{16,8},{24,16},{1,25},{9,1},{17,9},{25,17},{2,26},{10... | collective-permute-start | bytes 983048 | tf_op jit(solution)/shard_map/ppermute | solution.py:330
  240.1 8.4 %collective-permute-done.56 = bf16[256,640]{1,0:T(8,128)(2,1)S(1)} collective-permute-done((bf16[256,640]{1,0:T(8,128)(2,1)S(1)}, bf16[256,640]{1,0:T(8,128)(2,1)S(1)}, u32[]{:S(2)}, u32[]{:S(2)}) %collective-permute-start.56) | collective-permute-done | bytes 327712 | tf_op jit(solution)/shard_map/ppermute | solution.py:330
  250.8 3.1 collective-permute-start.26
  254.6 2.2 collective-permute-done.26
  259.0 15.5 %collective-permute-done.27 = bf16[40,960]{1,0:T(8,128)(2,1)S(1)} collective-permute-done((bf16[40,960]{1,0:T(8,128)(2,1)S(1)}, bf16[40,960]{1,0:T(8,128)(2,1)S(1)}, u32[]{:S(2)}, u32[]{:S(2)}) %collective-permute-start.27) | collective-permute-done | bytes 76832 | tf_op jit(solution)/shard_map/ppermute | solution.py:389
  274.6 2.8 collective-permute-start.59
  284.4 3.3 collective-permute-done.28
  288.7 2.7 collective-permute-start.61
  297.2 3.1 collective-permute-start.31
  302.6 10.8 %collective-permute-done.38 = bf16[480,640]{1,0:T(8,128)(2,1)S(1)} collective-permute-done((bf16[480,640]{1,0:T(8,128)(2,1)S(1)}, bf16[480,640]{1,0:T(8,128)(2,1)S(1)}, u32[]{:S(2)}, u32[]{:S(2)}) %collective-permute-start.38) | collective-permute-done | bytes 614432 | tf_op jit(solution)/shard_map/ppermute | solution.py:330
  313.8 8.1 %collective-permute-start.41 = (bf16[120,640]{1,0:T(8,128)(2,1)S(1)}, bf16[120,640]{1,0:T(8,128)(2,1)S(1)}, u32[]{:S(2)}, u32[]{:S(2)}) collective-permute-start(bf16[120,640]{1,0:T(8,128)(2,1)S(1)} %get-tuple-element.162), channel_id=1, source_target_pairs={{0,8},{8,16},{16,24},{24,0},{1,9},{9,17},{17,25},{25,1},{2,10},{10... | collective-permute-start | bytes 460808 | tf_op jit(solution)/shard_map/ppermute | solution.py:330
  325.4 2.8 collective-permute-done.41
  328.9 2.4 collective-permute-start.63
  333.4 2.4 collective-permute-start.44
  335.8 4.3 %collective-permute-done.44 = bf16[120,640]{1,0:T(8,128)(2,1)S(1)} collective-permute-done((bf16[120,640]{1,0:T(8,128)(2,1)S(1)}, bf16[120,640]{1,0:T(8,128)(2,1)S(1)}, u32[]{:S(2)}, u32[]{:S(2)}) %collective-permute-start.44) | collective-permute-done | bytes 153632 | tf_op jit(solution)/shard_map/ppermute | solution.py:389
  340.3 2.8 collective-permute-start.45
  343.1 4.4 %collective-permute-done.45 = bf16[120,640]{1,0:T(8,128)(2,1)S(1)} collective-permute-done((bf16[120,640]{1,0:T(8,128)(2,1)S(1)}, bf16[120,640]{1,0:T(8,128)(2,1)S(1)}, u32[]{:S(2)}, u32[]{:S(2)}) %collective-permute-start.45) | collective-permute-done | bytes 153632 | tf_op jit(solution)/shard_map/ppermute | solution.py:330
  349.6 3.9 collective-permute-done.46
  353.5 2.3 collective-permute-start.47
  355.8 4.5 %collective-permute-done.47 = bf16[120,640]{1,0:T(8,128)(2,1)S(1)} collective-permute-done((bf16[120,640]{1,0:T(8,128)(2,1)S(1)}, bf16[120,640]{1,0:T(8,128)(2,1)S(1)}, u32[]{:S(2)}, u32[]{:S(2)}) %collective-permute-start.47) | collective-permute-done | bytes 153632 | tf_op jit(solution)/shard_map/ppermute | solution.py:330
  365.8 2.8 collective-permute-start.66
  369.1 3.0 copy.118
  373.3 3.3 collective-permute-done.66.refs_10_
  380.3 6.3 %place_gradients.1 = (f32[240,960]{1,0:T(8,128)}, f32[240,320]{1,0:T(8,128)}, f32[240,320]{1,0:T(8,128)}, f32[240,960]{1,0:T(8,128)}, f32[8,256]{1,0:T(8,128)S(1...) custom-call(s32[2]{0:T(128)S(1)} %pad_add_fusion.place_ref, bf16[160,960]{1,0:T(8,128)(2,1)S(1)} %bitcast.117, ...), custom_call_target="tpu_custom_call" | custom-call | bytes 14835720 | tf_op jit(solution)/shard_map/place_gradients/pallas_call | solution.py:313
  386.6 3.2 copy.121
  (240 shorter events, 96.8 us)
Async XLA Ops:
  2.0 19.8 %collective-permute-start = (bf16[2,240]{1,0:T(2,128)(2,1)S(1)}, bf16[2,240]{1,0:T(2,128)(2,1)S(1)}, u32[]{:S(2)}, u32[]{:S(2)}) collective-permute-start(bf16[2,240]{1,0:T(2,128)(2,1)S(1)} %pad_maximum_fusion.4), channel_id=1, source_target_pairs={{0,64},{64,1},{1,65},{65,0},{2,66},{66,3},{3,67},{67,2},{4,68},{68... | collective-permute-start | bytes 2888 | tf_op jit(solution)/shard_map/ppermute | solution.py:335
  9.0 16.8 %collective-permute-start.4 = (bf16[112,2624]{1,0:T(8,128)(2,1)}, bf16[112,2624]{1,0:T(8,128)(2,1)}, u32[]{:S(2)}, u32[]{:S(2)}) collective-permute-start(bf16[112,2624]{1,0:T(8,128)(2,1)} %slice.71), channel_id=1, source_target_pairs={{0,65},{64,0},{1,64},{65,1},{2,67},{66,2},{3,66},{67,3},{4,69},{68... | collective-permute-start | bytes 1763336 | tf_op jit(solution)/shard_map/ppermute | solution.py:335
  12.4 17.1 %collective-permute-start.13 = (bf16[320,960]{1,0:T(8,128)(2,1)}, bf16[320,960]{1,0:T(8,128)(2,1)}, u32[]{:S(2)}, u32[]{:S(2)}) collective-permute-start(bf16[320,960]{1,0:T(8,128)(2,1)} %get-tuple-element.161), channel_id=1, source_target_pairs={{0,64},{64,1},{1,65},{65,0},{2,66},{66,3},{3,67},{67,2},{4,68},{68... | collective-permute-start | bytes 1843208 | tf_op jit(solution)/shard_map/ppermute | solution.py:335
  14.0 25.9 %collective-permute-start.14 = (bf16[320,960]{1,0:T(8,128)(2,1)S(1)}, bf16[320,960]{1,0:T(8,128)(2,1)}, u32[]{:S(2)}, u32[]{:S(2)}) collective-permute-start(bf16[320,960]{1,0:T(8,128)(2,1)S(1)} %get-tuple-element.160), channel_id=1, source_target_pairs={{0,65},{64,0},{1,64},{65,1},{2,67},{66,2},{3,66},{67,3},{4,69},{68... | collective-permute-start | bytes 1843208 | tf_op jit(solution)/shard_map/ppermute | solution.py:335
  19.0 52.1 %collective-permute-start.9 = (bf16[112,5120]{1,0:T(8,128)(2,1)}, bf16[112,5120]{1,0:T(8,128)(2,1)}, u32[]{:S(2)}, u32[]{:S(2)}) collective-permute-start(bf16[112,5120]{1,0:T(8,128)(2,1)} %slice.73), channel_id=1, source_target_pairs={{0,65},{64,0},{1,64},{65,1},{2,67},{66,2},{3,66},{67,3},{4,69},{68... | collective-permute-start | bytes 3440648 | tf_op jit(solution)/shard_map/ppermute | solution.py:335
  24.4 47.6 %collective-permute-start.8 = (bf16[128,5120]{1,0:T(8,128)(2,1)}, bf16[128,5120]{1,0:T(8,128)(2,1)}, u32[]{:S(2)}, u32[]{:S(2)}) collective-permute-start(bf16[128,5120]{1,0:T(8,128)(2,1)} %slice.72), channel_id=1, source_target_pairs={{0,64},{64,1},{1,65},{65,0},{2,66},{66,3},{3,67},{67,2},{4,68},{68... | collective-permute-start | bytes 3932168 | tf_op jit(solution)/shard_map/ppermute | solution.py:335
  25.9 79.5 %collective-permute-start.7 = (bf16[240,5120]{1,0:T(8,128)(2,1)}, bf16[240,5120]{1,0:T(8,128)(2,1)}, u32[]{:S(2)}, u32[]{:S(2)}) collective-permute-start(bf16[240,5120]{1,0:T(8,128)(2,1)} %constant_dynamic-update-slice_fusion.refs_0_.refs_6_), channel_id=1, source_target_pairs={{0,32},{32,0},{1,33},{33,1},{2,34},{34,2},{3,35},{35,3},{4,36},{36... | collective-permute-start | bytes 7372808 | tf_op jit(solution)/shard_map/ppermute | solution.py:326
  29.5 41.6 %collective-permute-start.3 = (bf16[128,2624]{0,1:T(8,128)(2,1)S(1)}, bf16[128,2624]{0,1:T(8,128)(2,1)}, u32[]{:S(2)}, u32[]{:S(2)}) collective-permute-start(bf16[128,2624]{0,1:T(8,128)(2,1)S(1)} %copy.98), channel_id=1, source_target_pairs={{0,64},{64,1},{1,65},{65,0},{2,66},{66,3},{3,67},{67,2},{4,68},{68... | collective-permute-start | bytes 2015240 | tf_op jit(solution)/shard_map/ppermute | solution.py:335
  39.9 35.3 %collective-permute-start.12 = (bf16[640,960]{0,1:T(8,128)(2,1)}, bf16[640,960]{0,1:T(8,128)(2,1)}, u32[]{:S(2)}, u32[]{:S(2)}) collective-permute-start(bf16[640,960]{0,1:T(8,128)(2,1)} %param.24), channel_id=1, source_target_pairs={{0,32},{32,0},{1,33},{33,1},{2,34},{34,2},{3,35},{35,3},{4,36},{36... | collective-permute-start | bytes 3686408 | tf_op jit(solution)/shard_map/ppermute | solution.py:326
  71.1 13.4 %collective-permute-start.2 = (bf16[240,2624]{1,0:T(8,128)(2,1)S(1)}, bf16[240,2624]{1,0:T(8,128)(2,1)}, u32[]{:S(2)}, u32[]{:S(2)}) collective-permute-start(bf16[240,2624]{1,0:T(8,128)(2,1)S(1)} %concatenate.23.refs_0_), channel_id=1, source_target_pairs={{0,32},{32,0},{1,33},{33,1},{2,34},{34,2},{3,35},{35,3},{4,36},{36... | collective-permute-start | bytes 3778568 | tf_op jit(solution)/shard_map/ppermute | solution.py:326
  72.0 33.4 %collective-permute-start.10 = (bf16[128,5120]{1,0:T(8,128)(2,1)}, bf16[128,5120]{1,0:T(8,128)(2,1)}, u32[]{:S(2)}, u32[]{:S(2)}) collective-permute-start(bf16[128,5120]{1,0:T(8,128)(2,1)} %collective-permute-done.8.refs_2_.refs_8_), channel_id=1, source_target_pairs={{0,32},{32,0},{1,33},{33,1},{2,34},{34,2},{3,35},{35,3},{4,36},{36... | collective-permute-start | bytes 3932168 | tf_op jit(solution)/shard_map/ppermute | solution.py:326
  75.2 30.2 %collective-permute-start.11 = (bf16[112,5120]{1,0:T(8,128)(2,1)}, bf16[112,5120]{1,0:T(8,128)(2,1)}, u32[]{:S(2)}, u32[]{:S(2)}) collective-permute-start(bf16[112,5120]{1,0:T(8,128)(2,1)} %collective-permute-done.9.refs_3_.refs_9_), channel_id=1, source_target_pairs={{0,32},{32,0},{1,33},{33,1},{2,34},{34,2},{3,35},{35,3},{4,36},{36... | collective-permute-start | bytes 3440648 | tf_op jit(solution)/shard_map/ppermute | solution.py:326
  84.1 37.9 %collective-permute-start.15 = (bf16[320,960]{1,0:T(8,128)(2,1)}, bf16[320,960]{1,0:T(8,128)(2,1)}, u32[]{:S(2)}, u32[]{:S(2)}) collective-permute-start(bf16[320,960]{1,0:T(8,128)(2,1)} %collective-permute-done.13.refs_2_), channel_id=1, source_target_pairs={{0,32},{32,0},{1,33},{33,1},{2,34},{34,2},{3,35},{35,3},{4,36},{36... | collective-permute-start | bytes 1843208 | tf_op jit(solution)/shard_map/ppermute | solution.py:326
  84.5 37.4 %collective-permute-start.16 = (bf16[320,960]{1,0:T(8,128)(2,1)}, bf16[320,960]{1,0:T(8,128)(2,1)}, u32[]{:S(2)}, u32[]{:S(2)}) collective-permute-start(bf16[320,960]{1,0:T(8,128)(2,1)} %collective-permute-done.14.refs_3_), channel_id=1, source_target_pairs={{0,32},{32,0},{1,33},{33,1},{2,34},{34,2},{3,35},{35,3},{4,36},{36... | collective-permute-start | bytes 1843208 | tf_op jit(solution)/shard_map/ppermute | solution.py:326
  121.0 57.8 %collective-permute-start.18 = (bf16[4,160,960]{2,1,0:T(8,128)(2,1)}, bf16[4,160,960]{2,1,0:T(8,128)(2,1)}, u32[]{:S(2)}, u32[]{:S(2)}) collective-permute-start(bf16[4,160,960]{2,1,0:T(8,128)(2,1)} %bitcast.152), channel_id=1, source_target_pairs={{0,32},{32,0},{1,33},{33,1},{2,34},{34,2},{3,35},{35,3},{4,36},{36... | collective-permute-start | bytes 3686408 | tf_op jit(solution)/shard_map/ppermute | solution.py:326
  165.1 18.1 %collective-permute-start.52 = (bf16[4,256,640]{2,1,0:T(8,128)(2,1)}, bf16[4,256,640]{2,1,0:T(8,128)(2,1)}, u32[]{:S(2)}, u32[]{:S(2)}) collective-permute-start(bf16[4,256,640]{2,1,0:T(8,128)(2,1)} %get-tuple-element.86), channel_id=1, source_target_pairs={{0,32},{32,0},{1,33},{33,1},{2,34},{34,2},{3,35},{35,3},{4,36},{36... | collective-permute-start | bytes 3932168 | tf_op jit(solution)/shard_map/ppermute | solution.py:326
  165.5 41.0 %collective-permute-start.51 = (bf16[4,256,640]{2,1,0:T(8,128)(2,1)}, bf16[4,256,640]{2,1,0:T(8,128)(2,1)}, u32[]{:S(2)}, u32[]{:S(2)}) collective-permute-start(bf16[4,256,640]{2,1,0:T(8,128)(2,1)} %get-tuple-element.84), channel_id=1, source_target_pairs={{0,32},{32,0},{1,33},{33,1},{2,34},{34,2},{3,35},{35,3},{4,36},{36... | collective-permute-start | bytes 3932168 | tf_op jit(solution)/shard_map/ppermute | solution.py:326
  166.0 21.4 %collective-permute-start.17 = (bf16[4,160,960]{2,1,0:T(8,128)(2,1)}, bf16[4,160,960]{2,1,0:T(8,128)(2,1)}, u32[]{:S(2)}, u32[]{:S(2)}) collective-permute-start(bf16[4,160,960]{2,1,0:T(8,128)(2,1)} %bitcast.15), channel_id=1, source_target_pairs={{0,32},{32,0},{1,33},{33,1},{2,34},{34,2},{3,35},{35,3},{4,36},{36... | collective-permute-start | bytes 3686408 | tf_op jit(solution)/shard_map/ppermute | solution.py:326
  178.4 57.4 %collective-permute-start.35 = (bf16[4,480,640]{2,1,0:T(8,128)(2,1)}, bf16[4,480,640]{2,1,0:T(8,128)(2,1)S(1)}, u32[]{:S(2)}, u32[]{:S(2)}) collective-permute-start(bf16[4,480,640]{2,1,0:T(8,128)(2,1)} %get-tuple-element.77), channel_id=1, source_target_pairs={{0,32},{32,0},{1,33},{33,1},{2,34},{34,2},{3,35},{35,3},{4,36},{36... | collective-permute-start | bytes 7372808 | tf_op jit(solution)/shard_map/ppermute | solution.py:326
  181.6 18.6 %collective-permute-start.19 = (bf16[2,160,960]{2,1,0:T(8,128)(2,1)S(1)}, bf16[2,160,960]{2,1,0:T(8,128)(2,1)}, u32[]{:S(2)}, u32[]{:S(2)}) collective-permute-start(bf16[2,160,960]{2,1,0:T(8,128)(2,1)S(1)} %get-tuple-element.158), channel_id=1, source_target_pairs={{0,64},{64,1},{1,65},{65,0},{2,66},{66,3},{3,67},{67,2},{4,68},{68... | collective-permute-start | bytes 1843208 | tf_op jit(solution)/shard_map/ppermute | solution.py:335
  183.2 20.3 %collective-permute-start.20 = (bf16[2,160,960]{2,1,0:T(8,128)(2,1)}, bf16[2,160,960]{2,1,0:T(8,128)(2,1)}, u32[]{:S(2)}, u32[]{:S(2)}) collective-permute-start(bf16[2,160,960]{2,1,0:T(8,128)(2,1)} %get-tuple-element.159), channel_id=1, source_target_pairs={{0,65},{64,0},{1,64},{65,1},{2,67},{66,2},{3,66},{67,3},{4,69},{68... | collective-permute-start | bytes 1843208 | tf_op jit(solution)/shard_map/ppermute | solution.py:335
  187.4 26.2 %collective-permute-start.53 = (bf16[2,256,640]{2,1,0:T(8,128)(2,1)}, bf16[2,256,640]{2,1,0:T(8,128)(2,1)S(1)}, u32[]{:S(2)}, u32[]{:S(2)}) collective-permute-start(bf16[2,256,640]{2,1,0:T(8,128)(2,1)} %get-tuple-element.153), channel_id=1, source_target_pairs={{0,64},{64,1},{1,65},{65,0},{2,66},{66,3},{3,67},{67,2},{4,68},{68... | collective-permute-start | bytes 1966088 | tf_op jit(solution)/shard_map/ppermute | solution.py:335
  200.2 17.5 %collective-permute-start.54 = (bf16[2,256,640]{2,1,0:T(8,128)(2,1)}, bf16[2,256,640]{2,1,0:T(8,128)(2,1)}, u32[]{:S(2)}, u32[]{:S(2)}) collective-permute-start(bf16[2,256,640]{2,1,0:T(8,128)(2,1)} %get-tuple-element.154), channel_id=1, source_target_pairs={{0,65},{64,0},{1,64},{65,1},{2,67},{66,2},{3,66},{67,3},{4,69},{68... | collective-permute-start | bytes 1966088 | tf_op jit(solution)/shard_map/ppermute | solution.py:335
  203.5 85.2 %collective-permute-start.34 = (bf16[4,480,640]{2,1,0:T(8,128)(2,1)}, bf16[4,480,640]{2,1,0:T(8,128)(2,1)S(1)}, u32[]{:S(2)}, u32[]{:S(2)}) collective-permute-start(bf16[4,480,640]{2,1,0:T(8,128)(2,1)} %get-tuple-element.75), channel_id=1, source_target_pairs={{0,32},{32,0},{1,33},{33,1},{2,34},{34,2},{3,35},{35,3},{4,36},{36... | collective-permute-start | bytes 7372808 | tf_op jit(solution)/shard_map/ppermute | solution.py:326
  206.5 15.9 %collective-permute-start.21 = (bf16[160,960]{1,0:T(8,128)(2,1)S(1)}, bf16[160,960]{1,0:T(8,128)(2,1)S(1)}, u32[]{:S(2)}, u32[]{:S(2)}) collective-permute-start(bf16[160,960]{1,0:T(8,128)(2,1)S(1)} %get-tuple-element.155), channel_id=1, source_target_pairs={{0,8},{8,16},{16,24},{24,0},{1,9},{9,17},{17,25},{25,1},{2,10},{10... | collective-permute-start | bytes 921608 | tf_op jit(solution)/shard_map/ppermute | solution.py:330
  213.6 17.9 %collective-permute-start.22 = (bf16[160,960]{1,0:T(8,128)(2,1)S(1)}, bf16[160,960]{1,0:T(8,128)(2,1)S(1)}, u32[]{:S(2)}, u32[]{:S(2)}) collective-permute-start(bf16[160,960]{1,0:T(8,128)(2,1)S(1)} %get-tuple-element.157), channel_id=1, source_target_pairs={{0,24},{8,0},{16,8},{24,16},{1,25},{9,1},{17,9},{25,17},{2,26},{10... | collective-permute-start | bytes 921608 | tf_op jit(solution)/shard_map/ppermute | solution.py:330
  217.6 17.9 %collective-permute-start.23 = (bf16[160,960]{1,0:T(8,128)(2,1)S(1)}, bf16[160,960]{1,0:T(8,128)(2,1)S(1)}, u32[]{:S(2)}, u32[]{:S(2)}) collective-permute-start(bf16[160,960]{1,0:T(8,128)(2,1)S(1)} %get-tuple-element.156), channel_id=1, source_target_pairs={{0,16},{8,24},{16,0},{24,8},{1,17},{9,25},{17,1},{25,9},{2,18},{10... | collective-permute-start | bytes 921608 | tf_op jit(solution)/shard_map/ppermute | solution.py:330
  222.4 15.9 %collective-permute-start.55 = (bf16[256,640]{1,0:T(8,128)(2,1)S(1)}, bf16[256,640]{1,0:T(8,128)(2,1)S(1)}, u32[]{:S(2)}, u32[]{:S(2)}) collective-permute-start(bf16[256,640]{1,0:T(8,128)(2,1)S(1)} %get-tuple-element.150), channel_id=1, source_target_pairs={{0,8},{8,16},{16,24},{24,0},{1,9},{9,17},{17,25},{25,1},{2,10},{10... | collective-permute-start | bytes 983048 | tf_op jit(solution)/shard_map/ppermute | solution.py:330
  231.5 17.0 %collective-permute-start.56 = (bf16[256,640]{1,0:T(8,128)(2,1)S(1)}, bf16[256,640]{1,0:T(8,128)(2,1)S(1)}, u32[]{:S(2)}, u32[]{:S(2)}) collective-permute-start(bf16[256,640]{1,0:T(8,128)(2,1)S(1)} %get-tuple-element.152), channel_id=1, source_target_pairs={{0,24},{8,0},{16,8},{24,16},{1,25},{9,1},{17,9},{25,17},{2,26},{10... | collective-permute-start | bytes 983048 | tf_op jit(solution)/shard_map/ppermute | solution.py:330
  235.6 13.0 %collective-permute-start.57 = (bf16[256,640]{1,0:T(8,128)(2,1)S(1)}, bf16[256,640]{1,0:T(8,128)(2,1)S(1)}, u32[]{:S(2)}, u32[]{:S(2)}) collective-permute-start(bf16[256,640]{1,0:T(8,128)(2,1)S(1)} %get-tuple-element.151), channel_id=1, source_target_pairs={{0,16},{8,24},{16,0},{24,8},{1,17},{9,25},{17,1},{25,9},{2,18},{10... | collective-permute-start | bytes 983048 | tf_op jit(solution)/shard_map/ppermute | solution.py:330
  235.8 14.9 %collective-permute-start.24 = (bf16[40,960]{1,0:T(8,128)(2,1)S(1)}, bf16[40,960]{1,0:T(8,128)(2,1)S(1)}, u32[]{:S(2)}, u32[]{:S(2)}) collective-permute-start(bf16[40,960]{1,0:T(8,128)(2,1)S(1)} %get-tuple-element.168), channel_id=1, source_target_pairs={{0,2},{2,4},{4,6},{6,0},{1,3},{3,5},{5,7},{7,1},{8,10},{10,12},{12... | collective-permute-start | bytes 230408 | tf_op jit(solution)/shard_map/ppermute | solution.py:330
  238.3 15.6 %collective-permute-start.25 = (bf16[40,960]{1,0:T(8,128)(2,1)S(1)}, bf16[40,960]{1,0:T(8,128)(2,1)S(1)}, u32[]{:S(2)}, u32[]{:S(2)}) collective-permute-start(bf16[40,960]{1,0:T(8,128)(2,1)S(1)} %get-tuple-element.170), channel_id=1, source_target_pairs={{0,6},{2,0},{4,2},{6,4},{1,7},{3,1},{5,3},{7,5},{8,14},{10,8},{12,... | collective-permute-start | bytes 230408 | tf_op jit(solution)/shard_map/ppermute | solution.py:330
  248.5 42.8 %collective-permute-start.36 = (bf16[2,480,640]{2,1,0:T(8,128)(2,1)S(1)}, bf16[2,480,640]{2,1,0:T(8,128)(2,1)S(1)}, u32[]{:S(2)}, u32[]{:S(2)}) collective-permute-start(bf16[2,480,640]{2,1,0:T(8,128)(2,1)S(1)} %get-tuple-element.148), channel_id=1, source_target_pairs={{0,64},{64,1},{1,65},{65,0},{2,66},{66,3},{3,67},{67,2},{4,68},{68... | collective-permute-start | bytes 3686408 | tf_op jit(solution)/shard_map/ppermute | solution.py:335
  248.5 42.8 %collective-permute-start.37 = (bf16[2,480,640]{2,1,0:T(8,128)(2,1)S(1)}, bf16[2,480,640]{2,1,0:T(8,128)(2,1)S(1)}, u32[]{:S(2)}, u32[]{:S(2)}) collective-permute-start(bf16[2,480,640]{2,1,0:T(8,128)(2,1)S(1)} %get-tuple-element.149), channel_id=1, source_target_pairs={{0,65},{64,0},{1,64},{65,1},{2,67},{66,2},{3,66},{67,3},{4,69},{68... | collective-permute-start | bytes 3686408 | tf_op jit(solution)/shard_map/ppermute | solution.py:335
  253.9 23.4 %collective-permute-start.58 = (bf16[64,640]{1,0:T(8,128)(2,1)S(1)}, bf16[64,640]{1,0:T(8,128)(2,1)S(1)}, u32[]{:S(2)}, u32[]{:S(2)}) collective-permute-start(bf16[64,640]{1,0:T(8,128)(2,1)S(1)} %get-tuple-element.165), channel_id=1, source_target_pairs={{0,2},{2,4},{4,6},{6,0},{1,3},{3,5},{5,7},{7,1},{8,10},{10,12},{12... | collective-permute-start | bytes 245768 | tf_op jit(solution)/shard_map/ppermute | solution.py:330
  256.9 17.7 %collective-permute-start.27 = (bf16[40,960]{1,0:T(8,128)(2,1)S(1)}, bf16[40,960]{1,0:T(8,128)(2,1)S(1)}, u32[]{:S(2)}, u32[]{:S(2)}) collective-permute-start(bf16[40,960]{1,0:T(8,128)(2,1)S(1)} %fusion.20), channel_id=1, source_target_pairs={{0,1},{1,0},{2,3},{3,2},{4,5},{5,4},{6,7},{7,6},{8,9},{9,8},{10,11... | collective-permute-start | bytes 230408 | tf_op jit(solution)/shard_map/ppermute | solution.py:389
  283.3 12.6 %collective-permute-start.29 = (bf16[40,960]{1,0:T(8,128)(2,1)S(1)}, bf16[40,960]{1,0:T(8,128)(2,1)S(1)}, u32[]{:S(2)}, u32[]{:S(2)}) collective-permute-start(bf16[40,960]{1,0:T(8,128)(2,1)S(1)} %get-tuple-element.144), channel_id=1, source_target_pairs={{0,6},{2,0},{4,2},{6,4},{1,7},{3,1},{5,3},{7,5},{8,14},{10,8},{12,... | collective-permute-start | bytes 230408 | tf_op jit(solution)/shard_map/ppermute | solution.py:330
  292.6 20.9 %collective-permute-start.38 = (bf16[480,640]{1,0:T(8,128)(2,1)S(1)}, bf16[480,640]{1,0:T(8,128)(2,1)S(1)}, u32[]{:S(2)}, u32[]{:S(2)}) collective-permute-start(bf16[480,640]{1,0:T(8,128)(2,1)S(1)} %get-tuple-element.145), channel_id=1, source_target_pairs={{0,2},{2,4},{4,6},{6,0},{1,3},{3,5},{5,7},{7,1},{8,10},{10,12},{12... | collective-permute-start | bytes 1843208 | tf_op jit(solution)/shard_map/ppermute | solution.py:330
  294.5 18.9 %collective-permute-start.39 = (bf16[480,640]{1,0:T(8,128)(2,1)S(1)}, bf16[480,640]{1,0:T(8,128)(2,1)S(1)}, u32[]{:S(2)}, u32[]{:S(2)}) collective-permute-start(bf16[480,640]{1,0:T(8,128)(2,1)S(1)} %get-tuple-element.147), channel_id=1, source_target_pairs={{0,6},{2,0},{4,2},{6,4},{1,7},{3,1},{5,3},{7,5},{8,14},{10,8},{12,... | collective-permute-start | bytes 1843208 | tf_op jit(solution)/shard_map/ppermute | solution.py:330
  295.9 17.6 %collective-permute-start.40 = (bf16[480,640]{1,0:T(8,128)(2,1)S(1)}, bf16[480,640]{1,0:T(8,128)(2,1)S(1)}, u32[]{:S(2)}, u32[]{:S(2)}) collective-permute-start(bf16[480,640]{1,0:T(8,128)(2,1)S(1)} %get-tuple-element.146), channel_id=1, source_target_pairs={{0,4},{2,6},{4,0},{6,2},{1,5},{3,7},{5,1},{7,3},{8,12},{10,14},{12... | collective-permute-start | bytes 1843208 | tf_op jit(solution)/shard_map/ppermute | solution.py:330
  297.2 64.9 %collective-permute-start.31 = (bf16[160,960]{1,0:T(8,128)(2,1)S(1)}, bf16[160,960]{1,0:T(8,128)(2,1)S(1)}, u32[]{:S(2)}, u32[]{:S(2)}) collective-permute-start(bf16[160,960]{1,0:T(8,128)(2,1)S(1)} %bitcast.114), channel_id=1, source_target_pairs={{0,8},{8,16},{16,24},{24,0},{1,9},{9,17},{17,25},{25,1},{2,10},{10... | collective-permute-start | bytes 921608 | tf_op jit(solution)/shard_map/ppermute | solution.py:330
  300.3 63.8 %collective-permute-start.32 = (bf16[160,960]{1,0:T(8,128)(2,1)S(1)}, bf16[160,960]{1,0:T(8,128)(2,1)S(1)}, u32[]{:S(2)}, u32[]{:S(2)}) collective-permute-start(bf16[160,960]{1,0:T(8,128)(2,1)S(1)} %bitcast.115), channel_id=1, source_target_pairs={{0,24},{8,0},{16,8},{24,16},{1,25},{9,1},{17,9},{25,17},{2,26},{10... | collective-permute-start | bytes 921608 | tf_op jit(solution)/shard_map/ppermute | solution.py:330
  313.8 14.4 %collective-permute-start.41 = (bf16[120,640]{1,0:T(8,128)(2,1)S(1)}, bf16[120,640]{1,0:T(8,128)(2,1)S(1)}, u32[]{:S(2)}, u32[]{:S(2)}) collective-permute-start(bf16[120,640]{1,0:T(8,128)(2,1)S(1)} %get-tuple-element.162), channel_id=1, source_target_pairs={{0,8},{8,16},{16,24},{24,0},{1,9},{9,17},{17,25},{25,1},{2,10},{10... | collective-permute-start | bytes 460808 | tf_op jit(solution)/shard_map/ppermute | solution.py:330
  328.2 37.5 %collective-permute-start.33 = (bf16[160,960]{1,0:T(8,128)(2,1)S(1)}, bf16[160,960]{1,0:T(8,128)(2,1)S(1)}, u32[]{:S(2)}, u32[]{:S(2)}) collective-permute-start(bf16[160,960]{1,0:T(8,128)(2,1)S(1)} %bitcast.116), channel_id=1, source_target_pairs={{0,16},{8,24},{16,0},{24,8},{1,17},{9,25},{17,1},{25,9},{2,18},{10... | collective-permute-start | bytes 921608 | tf_op jit(solution)/shard_map/ppermute | solution.py:330
  343.0 25.5 %collective-permute-start.65 = (bf16[256,640]{1,0:T(8,128)(2,1)S(1)}, bf16[256,640]{1,0:T(8,128)(2,1)S(1)}, u32[]{:S(2)}, u32[]{:S(2)}) collective-permute-start(bf16[256,640]{1,0:T(8,128)(2,1)S(1)} %bitcast.118), channel_id=1, source_target_pairs={{0,8},{8,16},{16,24},{24,0},{1,9},{9,17},{17,25},{25,1},{2,10},{10... | collective-permute-start | bytes 983048 | tf_op jit(solution)/shard_map/ppermute | solution.py:330
  360.4 16.9 %collective-permute-start.48 = (bf16[480,640]{1,0:T(8,128)(2,1)S(1)}, bf16[480,640]{1,0:T(8,128)(2,1)}, u32[]{:S(2)}, u32[]{:S(2)}) collective-permute-start(bf16[480,640]{1,0:T(8,128)(2,1)S(1)} %bitcast.129), channel_id=1, source_target_pairs={{0,2},{2,4},{4,6},{6,0},{1,3},{3,5},{5,7},{7,1},{8,10},{10,12},{12... | collective-permute-start | bytes 1843208 | tf_op jit(solution)/shard_map/ppermute | solution.py:330
  362.2 16.2 %collective-permute-start.49 = (bf16[480,640]{1,0:T(8,128)(2,1)S(1)}, bf16[480,640]{1,0:T(8,128)(2,1)}, u32[]{:S(2)}, u32[]{:S(2)}) collective-permute-start(bf16[480,640]{1,0:T(8,128)(2,1)S(1)} %bitcast.130), channel_id=1, source_target_pairs={{0,6},{2,0},{4,2},{6,4},{1,7},{3,1},{5,3},{7,5},{8,14},{10,8},{12,... | collective-permute-start | bytes 1843208 | tf_op jit(solution)/shard_map/ppermute | solution.py:330
  364.1 16.2 %collective-permute-start.50 = (bf16[480,640]{1,0:T(8,128)(2,1)S(1)}, bf16[480,640]{1,0:T(8,128)(2,1)}, u32[]{:S(2)}, u32[]{:S(2)}) collective-permute-start(bf16[480,640]{1,0:T(8,128)(2,1)S(1)} %bitcast.131), channel_id=1, source_target_pairs={{0,4},{2,6},{4,0},{6,2},{1,5},{3,7},{5,1},{7,3},{8,12},{10,14},{12... | collective-permute-start | bytes 1843208 | tf_op jit(solution)/shard_map/ppermute | solution.py:330
  (44 other events, 491.4 us)
